TPU v7x, 512 devices: a whole 4x8x8 slice. The times are simulated.
512 devices in a mesh: tile: 64 (over x, y, core), fblk: 8 (over z).
Axes of the slice: x: 4, y: 8, z: 8, core: 2. Of those that a mesh axis runs over, the one named last changes fastest.
Arguments:
- planes: float32 [512, 1024, 128], P(('fblk', 'tile')), may hold values from -40000 to 40000
- widths: int32 [4], replicated, may hold values from 1 to 8, as said below
Outputs:
- peak_maps: float32 [4, 1024, 128], P(None, 'tile')
Inputs may be any that keep to these rules, and one draw needn't show every extreme that they name: `widths`: some kernel has width 8 in every draw.
All inputs are finite; a program needn't handle non-finite values.
Results may differ from a plain program's by a relative error of at most 0.0001.
Values sent between devices are 32-bit elements; how exact they have to be, the bound alone decides.
No kernel may reach another device: no remote copies, remote signals or barrier semaphores. Data moves between devices by JAX's collectives and lax.ppermute only.
A program may use at most 64 MiB of HBM per device.

v0:
```python
import jax
import jax.numpy as jnp
from jax import lax
from jax.sharding import PartitionSpec as P

KERNELS = 4
RAD = 8
MAXW = 8


SIGMAS = (1.0, 1.6, 2.3, 3.2)
EPSILON = 1e-06


def shifted(block, axis, distance):
    devices = range(lax.axis_size(axis))
    route = [(i - distance, i) for i in devices if i - distance in devices]
    return lax.ppermute(block, axis, route)


def with_halo(value, sides, width):
    for axis, dim in sides:
        peers, length = (lax.axis_size(axis), value.shape[dim])
        up = [(i, (i + 1) % peers) for i in range(peers - 1)]
        down = [(j, i) for i, j in up]
        last = lax.slice_in_dim(value, length - width, length, axis=dim)
        leading = lax.slice_in_dim(value, 0, width, axis=dim)
        before = lax.ppermute(last, axis, up)
        after = lax.ppermute(leading, axis, down)
        value = jnp.concatenate([before, value, after], axis=dim)
    return value


def kernel_for(sigma):
    offsets = jnp.arange(2 * RAD + 1).astype(jnp.float32) - RAD
    values = jnp.exp(-offsets * offsets / (2.0 * sigma * sigma))
    return values / jnp.sum(values)


def pad_along(values, along):
    margins = [(0, 0)] * values.ndim
    margins[along] = (RAD, RAD)
    return jnp.pad(values, margins)


def filter_along(padded, kernel, along):
    length = padded.shape[along] - 2 * RAD
    summed = jnp.zeros(lax.slice_in_dim(padded, 0, length, axis=along).shape, jnp.float32)
    for offset in range(2 * RAD + 1):
        summed = summed + kernel[offset] * lax.slice_in_dim(
            padded, offset, offset + length, axis=along
        )
    return summed


def boxcar(extended, width, channels):
    scale = 1.0 / jnp.sqrt(width.astype(jnp.float32))
    summed = jnp.zeros((channels,) + extended.shape[1:], jnp.float32)
    for offset in range(MAXW):
        weight = jnp.where(offset < width, 1.0, 0.0).astype(jnp.float32) * scale
        summed = summed + weight * extended[offset : offset + channels]
    return summed


def channel_peak(smoothed, sum_squares, cells):
    rms_values = jnp.sqrt(sum_squares / cells + EPSILON)
    return jnp.max(smoothed / rms_values[:, None, None], axis=0)


def body(planes, widths):
    relaid = lax.all_to_all(planes, "tile", split_axis=1, concat_axis=0, tiled=True)
    channels = relaid.shape[0]
    cells = relaid.shape[1] * lax.axis_size("tile") * relaid.shape[2]
    band_edge = shifted(relaid[: MAXW - 1], "fblk", -1)
    extended = jnp.concatenate([relaid, band_edge], axis=0)
    peak_list = []
    for kernel_id in range(KERNELS):
        kernel = kernel_for(SIGMAS[kernel_id])
        spectral = boxcar(extended, widths[kernel_id], channels)
        horizontal = filter_along(pad_along(spectral, 2), kernel, 2)
        bordered = with_halo(horizontal, (("tile", 1),), RAD)
        smoothed = filter_along(bordered, kernel, 1)
        sum_squares = lax.psum(jnp.sum(smoothed * smoothed, axis=(1, 2)), "tile")
        peak_list.append(channel_peak(smoothed, sum_squares, cells))
    return lax.pmax(jnp.stack(peak_list), "fblk")


def solution(mesh):
    placed = (P(("fblk", "tile"), None, None), P())
    return jax.shard_map(
        body, mesh=mesh, in_specs=placed, out_specs=P(None, "tile", None), check_vma=False
    )
```

profile of v0, /device:TPU:64, one launch (start us, length us, event | category | flops | bytes accessed | tf_op | source)
XLA Modules:
  0.0 334.0 jit_solution(15228907142696872255)
XLA Ops:
  0.0 10.7 %all-to-all-start = ((f32[1,1024,128]{2,0,1:T(1,128)}), f32[1,1024,128]{2,0,1:T(1,128)S(1)}, u32[]{:S(2)}, u32[]{:S(2)}) async-start(f32[1,1024,128]{2,0,1:T(1,128)} %bitcast.111), calls=%async_computation | async-start | bytes 1048576 | tf_op jit(solution)/shard_map/all_to_all | solution.py:71
  10.7 0.6 fusion.338
  34.4 0.6 fusion.321
  35.1 0.7 fusion.320
  35.7 0.6 fusion.319
  36.4 0.7 fusion.318
  37.1 0.6 broadcast_divide_fusion.3
  37.7 0.6 broadcast_divide_fusion.2
  38.3 0.6 broadcast_divide_fusion.1
  39.0 0.6 broadcast_divide_fusion
  39.6 0.7 fusion.340
  40.3 0.7 fusion.339
  41.1 0.7 fusion.337
  41.8 0.0 all-to-all-done
  41.8 1.9 collective-permute-start
  43.7 0.7 fusion.336
  44.4 3.8 %collective-permute-done = f32[7,16,128]{2,1,0:T(8,128)S(1)} collective-permute-done((f32[7,16,128]{2,1,0:T(8,128)S(1)}, f32[7,16,128]{2,1,0:T(8,128)S(1)}, u32[]{:S(2)}, u32[]{:S(2)}) %collective-permute-start) | collective-permute-done | bytes 57376 | tf_op jit(solution)/shard_map/ppermute | solution.py:18
  48.2 0.4 multiply_add_fusion.3
  48.6 0.3 multiply_add_fusion.2
  48.9 12.7 %fusion.230 = f32[64,16,128]{2,1,0:T(8,128)S(1)} fusion(f32[64,16,128]{2,1,0:T(8,128)S(1)} %multiply_add_fusion.2, f32[]{:T(128)} %bitcast.53, f32[]{:T(128)} %bitcast.52, f32[]{:T(128)} %bitcast.51, f32[]{:T(128)} %bitcast.50, f32[]{:T(128)} %bitcast.49, f32[]{:T(128)} %bitcast.48, f32[]{:T(128)} %bitcast.47, f32[]{:T(128)} %bitcast.46, f32[]{:T(128)} %bitcast.45, ...), kind=kLoop, calls=%fused_computation.418 | loop fusion | flops 4325376 | bytes 1048644 | tf_op jit(solution)/shard_map/add | solution.py:50
  61.6 1.3 collective-permute-start.3
  62.9 1.3 collective-permute-start.4
  64.2 0.3 multiply_add_fusion
  64.5 12.8 %fusion.294 = f32[64,16,128]{2,1,0:T(8,128)S(1)} fusion(f32[64,16,128]{2,1,0:T(8,128)S(1)} %multiply_add_fusion, f32[]{:T(128)} %bitcast.105, f32[]{:T(128)} %bitcast.104, f32[]{:T(128)} %bitcast.103, f32[]{:T(128)} %bitcast.102, f32[]{:T(128)} %bitcast.101, f32[]{:T(128)} %bitcast.100, f32[]{:T(128)} %bitcast.99, f32[]{:T(128)} %bitcast.98, f32[]{:T(128)} %bitcast.97, ...), kind=kLoop, calls=%fused_computation.482 | loop fusion | flops 4325376 | bytes 1048644 | tf_op jit(solution)/shard_map/add | solution.py:50
  77.3 4.9 %collective-permute-start.7 = (f32[64,8,128]{2,1,0:T(8,128)S(1)}, f32[64,8,128]{2,1,0:T(8,128)S(1)}, u32[]{:S(2)}, u32[]{:S(2)}) collective-permute-start(f32[64,8,128]{2,1,0:T(8,128)S(1)} %get-tuple-element.30), channel_id=1, source_target_pairs={{0,8},{8,16},{16,24},{24,32},{32,40},{40,48},{48,56},{56,64},{64,7... | collective-permute-start | bytes 786440 | tf_op jit(solution)/shard_map/ppermute | solution.py:28
  82.2 1.3 collective-permute-start.8
  83.5 0.3 multiply_add_fusion.1
  83.8 12.9 %fusion.262 = f32[64,16,128]{2,1,0:T(8,128)S(1)} fusion(f32[64,16,128]{2,1,0:T(8,128)S(1)} %multiply_add_fusion.1, f32[]{:T(128)} %bitcast.79, f32[]{:T(128)} %bitcast.78, f32[]{:T(128)} %bitcast.77, f32[]{:T(128)} %bitcast.76, f32[]{:T(128)} %bitcast.75, f32[]{:T(128)} %bitcast.74, f32[]{:T(128)} %bitcast.73, f32[]{:T(128)} %bitcast.72, f32[]{:T(128)} %bitcast.71, ...), kind=kLoop, calls=%fused_computation.450 | loop fusion | flops 4325376 | bytes 1048644 | tf_op jit(solution)/shard_map/add | solution.py:50
  96.8 4.3 %collective-permute-start.5 = (f32[64,8,128]{2,1,0:T(8,128)S(1)}, f32[64,8,128]{2,1,0:T(8,128)S(1)}, u32[]{:S(2)}, u32[]{:S(2)}) collective-permute-start(f32[64,8,128]{2,1,0:T(8,128)S(1)} %get-tuple-element.28), channel_id=1, source_target_pairs={{0,8},{8,16},{16,24},{24,32},{32,40},{40,48},{48,56},{56,64},{64,7... | collective-permute-start | bytes 786440 | tf_op jit(solution)/shard_map/ppermute | solution.py:28
  101.0 12.8 %fusion.198 = f32[64,16,128]{2,1,0:T(8,128)S(1)} fusion(f32[64,16,128]{2,1,0:T(8,128)S(1)} %get-tuple-element.11, f32[]{:T(128)} %bitcast.27, f32[]{:T(128)} %bitcast.26, f32[]{:T(128)} %bitcast.25, f32[]{:T(128)} %bitcast.24, f32[]{:T(128)} %bitcast.23, f32[]{:T(128)} %bitcast.22, f32[]{:T(128)} %bitcast.21, f32[]{:T(128)} %bitcast.20, f32[]{:T(128)} %bitcast.19, ...), kind=kLoop, calls=%fused_computation.386 | loop fusion | flops 4325376 | bytes 1048644 | tf_op jit(solution)/shard_map/add | solution.py:50
  113.9 1.3 collective-permute-start.6
  115.2 0.0 collective-permute-done.4
  115.2 4.4 %collective-permute-start.1 = (f32[64,8,128]{2,1,0:T(8,128)S(1)}, f32[64,8,128]{2,1,0:T(8,128)S(1)}, u32[]{:S(2)}, u32[]{:S(2)}) collective-permute-start(f32[64,8,128]{2,1,0:T(8,128)S(1)} %get-tuple-element.24), channel_id=1, source_target_pairs={{0,8},{8,16},{16,24},{24,32},{32,40},{40,48},{48,56},{56,64},{64,7... | collective-permute-start | bytes 786440 | tf_op jit(solution)/shard_map/ppermute | solution.py:28
  119.7 12.5 %multiply_reduce_fusion.2 = (f32[64]{0:T(128)S(1)}, f32[64,16,128]{2,1,0:T(8,128)S(1)}) fusion(f32[64,8,128]{2,1,0:T(8,128)S(1)} %collective-permute-done.4, f32[64,16,128]{2,1,0:T(8,128)S(1)} %fusion.230, f32[]{:T(128)} %bitcast.53, f32[]{:T(128)} %bitcast.52, f32[]{:T(128)} %bitcast.51, f32[]{:T(128)} %bitcast.50, f32[]{:T(128)} %bitcast.49, f32[]{:T(128)} %bitcast.48, ...), kind=kLoop, calls=%fused_computation.519 | loop fusion | flops 6684608 | bytes 1573188 | tf_op jit(solution)/shard_map/reduce_sum | solution.py:83
  132.2 0.0 collective-permute-done.7
  132.2 1.3 collective-permute-start.2
  133.5 0.0 collective-permute-done.8
  133.5 12.6 %multiply_reduce_fusion = (f32[64]{0:T(128)S(1)}, f32[64,16,128]{2,1,0:T(8,128)S(1)}) fusion(f32[64,8,128]{2,1,0:T(8,128)S(1)} %collective-permute-done.8, f32[64,16,128]{2,1,0:T(8,128)S(1)} %fusion.294, f32[]{:T(128)} %bitcast.105, f32[]{:T(128)} %bitcast.104, f32[]{:T(128)} %bitcast.103, f32[]{:T(128)} %bitcast.102, f32[]{:T(128)} %bitcast.101, ...), kind=kLoop, calls=%fused_computation.515 | loop fusion | flops 6684608 | bytes 1573188 | tf_op jit(solution)/shard_map/reduce_sum | solution.py:83
  146.1 0.0 collective-permute-done.6
  146.1 12.7 %multiply_reduce_fusion.1 = (f32[64]{0:T(128)S(1)}, f32[64,16,128]{2,1,0:T(8,128)S(1)}) fusion(f32[64,8,128]{2,1,0:T(8,128)S(1)} %collective-permute-done.6, f32[64,16,128]{2,1,0:T(8,128)S(1)} %fusion.262, f32[]{:T(128)} %bitcast.79, f32[]{:T(128)} %bitcast.78, f32[]{:T(128)} %bitcast.77, f32[]{:T(128)} %bitcast.76, f32[]{:T(128)} %bitcast.75, f32[]{:T(128)} %bitcast.74, ...), kind=kLoop, calls=%fused_computation.517 | loop fusion | flops 6684608 | bytes 1573188 | tf_op jit(solution)/shard_map/reduce_sum | solution.py:83
  158.8 0.0 collective-permute-done.2
  158.8 12.6 %multiply_reduce_fusion.3 = (f32[64]{0:T(128)S(1)}, f32[64,16,128]{2,1,0:T(8,128)S(1)}) fusion(f32[64,8,128]{2,1,0:T(8,128)S(1)} %collective-permute-done.2, f32[64,16,128]{2,1,0:T(8,128)S(1)} %fusion.198, f32[]{:T(128)} %bitcast.27, f32[]{:T(128)} %bitcast.26, f32[]{:T(128)} %bitcast.25, f32[]{:T(128)} %bitcast.24, f32[]{:T(128)} %bitcast.23, f32[]{:T(128)} %bitcast.22, ...), kind=kLoop, calls=%fused_computation.521 | loop fusion | flops 6684608 | bytes 1573188 | tf_op jit(solution)/shard_map/reduce_sum | solution.py:83
  171.5 130.0 %all-reduce.4 = (f32[64]{0:T(128)S(1)}, f32[64]{0:T(128)S(1)}, f32[64]{0:T(128)S(1)}, f32[64]{0:T(128)S(1)}) all-reduce(f32[64]{0:T(128)S(1)} %get-tuple-element.22, f32[64]{0:T(128)S(1)} %get-tuple-element.20, f32[64]{0:T(128)S(1)} %get-tuple-element.18, f32[64]{0:T(128)S(1)} %get-tuple-element.9), channel_id=1, replica_groups=mesh['tile'=64,'fblk'=8] {'tile'}, use_global_device_ids=true, to_apply=%region_14.15 | all-reduce | flops 256 | bytes 2048 | tf_op jit(solution)/shard_map/psum | solution.py:83
  301.5 0.1 divide_reduce_fusion.1
  301.6 0.1 divide_reduce_fusion
  301.8 0.1 divide_reduce_fusion.3
  302.0 0.1 divide_reduce_fusion.2
  302.1 31.9 %pmax.7 = f32[4,16,128]{2,1,0:T(8,128)} all-reduce(f32[4,16,128]{2,1,0:T(8,128)S(1)} %pad_maximum_fusion.9), channel_id=1, replica_groups=mesh['tile'=64,'fblk'=8] {'fblk'}, use_global_device_ids=true, to_apply=%region_16.17 | all-reduce | flops 8192 | bytes 65536 | tf_op jit(solution)/shard_map/pmax | solution.py:85
  (13 shorter events, 0.2 us)
Async XLA Ops:
  0.0 10.7 %copy-start = (s32[4]{0:T(128)S(1)}, s32[4]{0:T(128)}, u32[]{:S(2)}) copy-start(s32[4]{0:T(128)} %param.3) | copy-start | bytes 52
  0.0 41.8 %all-to-all-start = ((f32[1,1024,128]{2,0,1:T(1,128)}), f32[1,1024,128]{2,0,1:T(1,128)S(1)}, u32[]{:S(2)}, u32[]{:S(2)}) async-start(f32[1,1024,128]{2,0,1:T(1,128)} %bitcast.111), calls=%async_computation | async-start | bytes 1048576 | tf_op jit(solution)/shard_map/all_to_all | solution.py:71
  41.8 6.4 %collective-permute-start = (f32[7,16,128]{2,1,0:T(8,128)S(1)}, f32[7,16,128]{2,1,0:T(8,128)S(1)}, u32[]{:S(2)}, u32[]{:S(2)}) collective-permute-start(f32[7,16,128]{2,1,0:T(8,128)S(1)} %bitcast.112), channel_id=1, source_target_pairs={{1,0},{2,1},{3,2},{4,3},{5,4},{6,5},{7,6},{9,8},{10,9},{11,10},{12... | collective-permute-start | bytes 172040 | tf_op jit(solution)/shard_map/ppermute | solution.py:18
  61.6 52.3 %collective-permute-start.3 = (f32[64,8,128]{2,1,0:T(8,128)S(1)}, f32[64,8,128]{2,1,0:T(8,128)S(1)}, u32[]{:S(2)}, u32[]{:S(2)}) collective-permute-start(f32[64,8,128]{2,1,0:T(8,128)S(1)} %get-tuple-element.26), channel_id=1, source_target_pairs={{0,8},{8,16},{16,24},{24,32},{32,40},{40,48},{48,56},{56,64},{64,7... | collective-permute-start | bytes 786440 | tf_op jit(solution)/shard_map/ppermute | solution.py:28
  62.9 52.3 %collective-permute-start.4 = (f32[64,8,128]{2,1,0:T(8,128)S(1)}, f32[64,8,128]{2,1,0:T(8,128)S(1)}, u32[]{:S(2)}, u32[]{:S(2)}) collective-permute-start(f32[64,8,128]{2,1,0:T(8,128)S(1)} %get-tuple-element.27), channel_id=1, source_target_pairs={{8,0},{16,8},{24,16},{32,24},{40,32},{48,40},{56,48},{64,56},{72,6... | collective-permute-start | bytes 786440 | tf_op jit(solution)/shard_map/ppermute | solution.py:29
  77.3 54.9 %collective-permute-start.7 = (f32[64,8,128]{2,1,0:T(8,128)S(1)}, f32[64,8,128]{2,1,0:T(8,128)S(1)}, u32[]{:S(2)}, u32[]{:S(2)}) collective-permute-start(f32[64,8,128]{2,1,0:T(8,128)S(1)} %get-tuple-element.30), channel_id=1, source_target_pairs={{0,8},{8,16},{16,24},{24,32},{32,40},{40,48},{48,56},{56,64},{64,7... | collective-permute-start | bytes 786440 | tf_op jit(solution)/shard_map/ppermute | solution.py:28
  82.2 51.3 %collective-permute-start.8 = (f32[64,8,128]{2,1,0:T(8,128)S(1)}, f32[64,8,128]{2,1,0:T(8,128)S(1)}, u32[]{:S(2)}, u32[]{:S(2)}) collective-permute-start(f32[64,8,128]{2,1,0:T(8,128)S(1)} %get-tuple-element.31), channel_id=1, source_target_pairs={{8,0},{16,8},{24,16},{32,24},{40,32},{48,40},{56,48},{64,56},{72,6... | collective-permute-start | bytes 786440 | tf_op jit(solution)/shard_map/ppermute | solution.py:29
  96.8 49.3 %collective-permute-start.5 = (f32[64,8,128]{2,1,0:T(8,128)S(1)}, f32[64,8,128]{2,1,0:T(8,128)S(1)}, u32[]{:S(2)}, u32[]{:S(2)}) collective-permute-start(f32[64,8,128]{2,1,0:T(8,128)S(1)} %get-tuple-element.28), channel_id=1, source_target_pairs={{0,8},{8,16},{16,24},{24,32},{32,40},{40,48},{48,56},{56,64},{64,7... | collective-permute-start | bytes 786440 | tf_op jit(solution)/shard_map/ppermute | solution.py:28
  113.9 32.2 %collective-permute-start.6 = (f32[64,8,128]{2,1,0:T(8,128)S(1)}, f32[64,8,128]{2,1,0:T(8,128)S(1)}, u32[]{:S(2)}, u32[]{:S(2)}) collective-permute-start(f32[64,8,128]{2,1,0:T(8,128)S(1)} %get-tuple-element.29), channel_id=1, source_target_pairs={{8,0},{16,8},{24,16},{32,24},{40,32},{48,40},{56,48},{64,56},{72,6... | collective-permute-start | bytes 786440 | tf_op jit(solution)/shard_map/ppermute | solution.py:29
  115.2 43.6 %collective-permute-start.1 = (f32[64,8,128]{2,1,0:T(8,128)S(1)}, f32[64,8,128]{2,1,0:T(8,128)S(1)}, u32[]{:S(2)}, u32[]{:S(2)}) collective-permute-start(f32[64,8,128]{2,1,0:T(8,128)S(1)} %get-tuple-element.24), channel_id=1, source_target_pairs={{0,8},{8,16},{16,24},{24,32},{32,40},{40,48},{48,56},{56,64},{64,7... | collective-permute-start | bytes 786440 | tf_op jit(solution)/shard_map/ppermute | solution.py:28
  132.2 26.6 %collective-permute-start.2 = (f32[64,8,128]{2,1,0:T(8,128)S(1)}, f32[64,8,128]{2,1,0:T(8,128)S(1)}, u32[]{:S(2)}, u32[]{:S(2)}) collective-permute-start(f32[64,8,128]{2,1,0:T(8,128)S(1)} %get-tuple-element.25), channel_id=1, source_target_pairs={{8,0},{16,8},{24,16},{32,24},{40,32},{48,40},{56,48},{64,56},{72,6... | collective-permute-start | bytes 786440 | tf_op jit(solution)/shard_map/ppermute | solution.py:29
where the time goes:
time: 336 us; the launch traced here: 334 us
  blocking collectives  162 us (48%)
  other arithmetic  109 us (32%)
  starting transfers between devices  32.7 us (10%)
  between operations  23.4 us (7%)
  waiting for transfers between devices  3.8 us (1%)
  local copies, waits for them, and re-layouts  3.62 us (1%)
    psum x1, blocking collectives, body(): sum_squares = lax.psum(jnp.sum(smoothed * smoothed, axis=(1, 2)), 'tile')  130 us
    add x4, other arithmetic, filter_along(): summed + kernel[offset] * lax.slice_in_dim(padded, offset, offset + lengt...  51.2 us
    reduce_sum x4, other arithmetic, body(): sum_squares = lax.psum(jnp.sum(smoothed * smoothed, axis=(1, 2)), 'tile')  50.4 us
    pmax x1, blocking collectives, body(): return lax.pmax(jnp.stack(peak_list), 'fblk')  31.9 us
    ppermute x4, starting transfers between devices, with_halo(): before = lax.ppermute(last, axis, up)  14.9 us
    all_to_all x1, starting transfers between devices, body(): lax.all_to_all(planes, 'tile', split_axis=1, concat_axis=0, tiled=True)  10.7 us
  transfers between devices with their start and end apart: 10, of which 1 were waited for; matrix products, arithmetic and copies ran while one was open for 26% of the time, Pallas kernels for 0%

commit v1 on v0

v1 whole, which is shorter than its diff:
```python
import jax
import jax.numpy as jnp
import numpy as np
from jax import lax
from jax.experimental import pallas as pl
from jax.experimental.pallas import tpu as pltpu
from jax.sharding import PartitionSpec as P

KERNELS = 4
RAD = 8
MAXW = 8
SIGMAS = (1.0, 1.6, 2.3, 3.2)
EPSILON = 1e-06
ROWS = 16
SPAN = ROWS + 2 * RAD
GROUP = 8
NX = 128
BF = jnp.bfloat16
F32 = jnp.float32
VMEM = pl.BlockSpec(memory_space=pltpu.VMEM)
SMEM = pl.BlockSpec(memory_space=pltpu.SMEM)
PARAMS = pltpu.CompilerParams(vmem_limit_bytes=32 * 1024 * 1024)


def taps(sigma):
    offsets = np.arange(2 * RAD + 1) - RAD
    values = np.exp(-(offsets**2) / (2.0 * sigma * sigma))
    return values / values.sum()


def split(matrix):
    matrix = np.asarray(matrix, np.float32)
    high = matrix.astype(BF)
    return high, (matrix - high.astype(np.float32)).astype(BF)


def vertical_matrix():
    out = np.zeros((KERNELS, GROUP, ROWS, 2 * GROUP, SPAN))
    for k, sigma in enumerate(SIGMAS):
        weights = taps(sigma)
        for row in range(ROWS):
            for channel in range(GROUP):
                for offset in range(MAXW):
                    out[k, channel, row, channel + offset, row : row + 2 * RAD + 1] = weights
    return out.reshape(KERNELS * GROUP * ROWS, 2 * GROUP * SPAN)


def horizontal_matrices():
    out = np.zeros((KERNELS, 2, NX, 2, NX))
    for k, sigma in enumerate(SIGMAS):
        weights = taps(sigma)
        for x in range(NX):
            for j in range(-RAD, RAD + 1):
                if 0 <= x + j < NX:
                    out[k, :, x + j, :, x] = weights[j + RAD] * np.eye(2)
    return out.reshape(KERNELS, 2 * NX, 2 * NX)


def halves(values):
    high = values.astype(BF)
    return high, (values - high.astype(F32)).astype(BF)


def dot3(a_high, a_low, b_high, b_low):
    def dot(a, b):
        return jnp.dot(a, b, preferred_element_type=F32)

    return dot(a_high, b_high) + (dot(a_low, b_high) + dot(a_high, b_low))


def mask_kernel(widths, high_in, low_in, high, low):
    block = GROUP * ROWS
    shape = (block, 2 * GROUP * SPAN)
    offset = lax.broadcasted_iota(jnp.int32, shape, 1) // SPAN - lax.broadcasted_iota(jnp.int32, shape, 0) // ROWS
    for k in range(KERNELS):
        keep = jnp.where(offset < widths[k], 1.0, 0.0)
        rows = pl.ds(k * block, block)
        high[rows, :] = (high_in[rows, :].astype(F32) * keep).astype(BF)
        low[rows, :] = (low_in[rows, :].astype(F32) * keep).astype(BF)


def smooth_kernel(own, before, after, edge, a_high, a_low, h_high, h_low, smoothed, sums, x_high, x_low):
    channels = own.shape[0]
    x = jnp.concatenate([before[...], own[...], after[...]], axis=1)
    x_high[0:channels], x_low[0:channels] = halves(x)
    x = jnp.concatenate([edge[...], jnp.zeros((1, SPAN, NX), F32)], axis=0)
    x_high[channels:], x_low[channels:] = halves(x)
    block = GROUP * ROWS
    partial = [[None] * (channels // GROUP) for _ in range(KERNELS)]
    for pair in range(channels // (2 * GROUP)):

        def side_by_side(ref):
            first = 2 * pair * GROUP
            parts = [ref[first + s : first + s + 2 * GROUP].reshape(2 * GROUP * SPAN, NX) for s in (0, GROUP)]
            return jnp.concatenate(parts, axis=1)

        xh, xl = side_by_side(x_high), side_by_side(x_low)
        for k in range(KERNELS):
            rows = pl.ds(k * block, block)
            y = dot3(a_high[rows, :], a_low[rows, :], xh, xl)
            yh, yl = halves(y)
            z = dot3(yh, yl, h_high[k], h_low[k])
            smoothed[k, pair] = z
            squares = jnp.sum((z * z).reshape(GROUP, ROWS, 2 * NX), axis=1)
            partial[k][2 * pair] = squares[:, :NX]
            partial[k][2 * pair + 1] = squares[:, NX:]
    stacked = jnp.concatenate([p for row in partial for p in row], axis=0)
    total = lax.dot_general(
        jnp.ones((8, NX), F32), stacked, (((1,), (1,)), ((), ())), precision=lax.Precision.HIGHEST, preferred_element_type=F32
    )
    odd = lax.broadcasted_iota(jnp.int32, sums.shape, 0) % 2
    both = [jnp.broadcast_to(total[0:1, h * NX : (h + 1) * NX], sums.shape) for h in (0, 1)]
    sums[...] = jnp.where(odd == 0, both[0], both[1])


def peak_kernel(cells, copies, widths, received, smoothed, peaks, scale):
    lane_odd = lax.broadcasted_iota(jnp.int32, (received.shape[0], NX), 0) % 2
    values = received[...]
    per_half = 2 * NX // KERNELS
    for h in (0, 1):
        total = lax.dot_general(
            values,
            jnp.where(lane_odd == h, 1.0, 0.0),
            (((0,), (0,)), ((), ())),
            precision=lax.Precision.HIGHEST,
            preferred_element_type=F32,
        )
        for i in range(KERNELS // 2):
            k = h * (KERNELS // 2) + i
            part = total[i * per_half : (i + 1) * per_half]
            floor = widths[k].astype(F32) * EPSILON
            scale[k] = 1.0 / jnp.sqrt(part * (1.0 / cells) + floor)
    for k in range(KERNELS):
        best = None
        for pair in range(smoothed.shape[1]):
            for g in (0, 1):
                for c in range(GROUP):
                    index = (2 * pair + g) * GROUP + c
                    value = smoothed[k, pair, c * ROWS : (c + 1) * ROWS, g * NX : (g + 1) * NX]
                    value = value * scale[k, index : index + 1, :]
                    best = value if best is None else jnp.maximum(best, value)
        for i in range(copies):
            peaks[i, k] = best


def body(planes, widths):
    tiles, blocks = lax.axis_size("tile"), lax.axis_size("fblk")
    own = lax.all_to_all(planes, "tile", split_axis=1, concat_axis=0, tiled=True)
    channels = own.shape[0]
    cells = ROWS * tiles * NX
    a_high, a_low = map(jnp.asarray, split(vertical_matrix()))
    h_high, h_low = map(jnp.asarray, split(horizontal_matrices()))
    a_shape = jax.ShapeDtypeStruct(a_high.shape, BF)
    a_high, a_low = pl.pallas_call(
        mask_kernel, out_shape=[a_shape, a_shape], in_specs=[SMEM, VMEM, VMEM], out_specs=[VMEM, VMEM], compiler_params=PARAMS
    )(widths, a_high, a_low)
    up = [(i, i + 1) for i in range(tiles - 1)]
    down = [(i + 1, i) for i in range(tiles - 1)]
    before = lax.ppermute(own[:, ROWS - RAD :], "tile", up)
    after = lax.ppermute(own[:, :RAD], "tile", down)
    first = slice(0, MAXW - 1)
    edge = jnp.concatenate([before[first], own[first], after[first]], axis=1)
    edge = lax.ppermute(edge, "fblk", [(i + 1, i) for i in range(blocks - 1)])
    smoothed, sums = pl.pallas_call(
        smooth_kernel,
        out_shape=[
            jax.ShapeDtypeStruct((KERNELS, channels // (2 * GROUP), GROUP * ROWS, 2 * NX), F32),
            jax.ShapeDtypeStruct((2 * tiles, NX), F32),
        ],
        in_specs=[VMEM] * 8,
        out_specs=[VMEM] * 2,
        scratch_shapes=[pltpu.VMEM((channels + MAXW, SPAN, NX), BF)] * 2,
        compiler_params=PARAMS,
    )(own, before, after, edge, a_high, a_low, h_high, h_low)
    received = lax.all_to_all(sums, "tile", split_axis=0, concat_axis=0, tiled=True)
    peaks = pl.pallas_call(
        lambda *refs: peak_kernel(cells, blocks, *refs),
        out_shape=jax.ShapeDtypeStruct((blocks, KERNELS, ROWS, NX), F32),
        in_specs=[SMEM, VMEM, VMEM],
        out_specs=VMEM,
        scratch_shapes=[pltpu.VMEM((KERNELS, channels, NX), F32)],
        compiler_params=PARAMS,
    )(widths, received, smoothed)
    peaks = lax.all_to_all(peaks, "fblk", split_axis=0, concat_axis=0, tiled=True)
    return jnp.max(peaks, axis=0)


def solution(mesh):
    placed = (P(("fblk", "tile"), None, None), P())
    return jax.shard_map(body, mesh=mesh, in_specs=placed, out_specs=P(None, "tile", None), check_vma=False)
```

time: 336 us -> 93.8 us (0.28)
  the two profiles are of different devices: /device:TPU:64 before, /device:TPU:1 now
where the time goes in v1:
time: 93.8 us; the launch traced here: 93.5 us
  blocking collectives  70 us (75%)
  Pallas kernels  8.51 us (9%)
  waiting for transfers between devices  7.3 us (8%)
  starting transfers between devices  6.85 us (7%)
    all_to_all x1, blocking collectives, body(): lax.all_to_all(planes, 'tile', split_axis=1, concat_axis=0, tiled=True)  29.1 us
    all_to_all x1, blocking collectives, body(): lax.all_to_all(sums, 'tile', split_axis=0, concat_axis=0, tiled=True)  20.5 us
    all_to_all x1, blocking collectives, body(): lax.all_to_all(peaks, 'fblk', split_axis=0, concat_axis=0, tiled=True)  20.4 us
    pallas_call x1, Pallas kernels, body(): pl.pallas_call(smooth_kernel, out_shape=[jax.ShapeDtypeStruct((KERNELS, c...  6.65 us
    ppermute x1, waiting for transfers between devices, body(): edge = lax.ppermute(edge, 'fblk', [(i + 1, i) for i in range(blocks - 1)])  4.03 us
    ppermute x1, starting transfers between devices, body(): before = lax.ppermute(own[:, ROWS - RAD:], 'tile', up)  3.33 us
    ppermute x1, starting transfers between devices, body(): after = lax.ppermute(own[:, :RAD], 'tile', down)  2.23 us
    ppermute x1, waiting for transfers between devices, body(): after = lax.ppermute(own[:, :RAD], 'tile', down)  2.1 us
  transfers between devices with their start and end apart: 3, of which 3 were waited for; matrix products, arithmetic and copies ran while one was open for 0% of the time, Pallas kernels for 1%

profile of v1, /device:TPU:1, one launch (start us, length us, event | category | flops | bytes accessed | tf_op | source)
XLA Modules:
  0.0 93.5 jit_solution(3890021436769687538)
XLA Ops:
  0.0 0.0 copy-start.2
  0.0 0.0 copy-start.3
  0.0 0.0 copy-start
  0.0 0.0 copy-start.1
  0.0 0.0 copy-start.4
  0.0 29.1 %all_to_all.28 = f32[1,1024,128]{2,0,1:T(1,128)S(1)} all-to-all(f32[1,1024,128]{2,0,1:T(1,128)} %bitcast.9), channel_id=1, replica_groups=mesh['tile'=64,'fblk'=8] {'tile'}, dimensions={1} | all-to-all | bytes 1048576 | tf_op jit(solution)/shard_map/all_to_all | solution.py:148
  29.2 2.2 %collective-permute-start.1 = (f32[64,8,128]{2,1,0:T(8,128)S(1)}, f32[64,8,128]{2,1,0:T(8,128)S(1)}, u32[]{:S(2)}, u32[]{:S(2)}) collective-permute-start(f32[64,8,128]{2,1,0:T(8,128)S(1)} %get-tuple-element.13), channel_id=1, source_target_pairs={{8,0},{16,8},{24,16},{32,24},{40,32},{48,40},{56,48},{64,56},{72,6... | collective-permute-start | bytes 786440 | tf_op jit(solution)/shard_map/ppermute | solution.py:160
  31.4 3.3 %collective-permute-start = (f32[64,8,128]{2,1,0:T(8,128)S(1)}, f32[64,8,128]{2,1,0:T(8,128)S(1)}, u32[]{:S(2)}, u32[]{:S(2)}) collective-permute-start(f32[64,8,128]{2,1,0:T(8,128)S(1)} %get-tuple-element.14), channel_id=1, source_target_pairs={{0,8},{8,16},{16,24},{24,32},{32,40},{40,48},{48,56},{56,64},{64,7... | collective-permute-start | bytes 786440 | tf_op jit(solution)/shard_map/ppermute | solution.py:159
  34.7 2.1 %collective-permute-done.1.after = f32[64,8,128]{2,1,0:T(8,128)S(1)} collective-permute-done((f32[64,8,128]{2,1,0:T(8,128)S(1)}, f32[64,8,128]{2,1,0:T(8,128)S(1)}, u32[]{:S(2)}, u32[]{:S(2)}) %collective-permute-start.1) | collective-permute-done | bytes 262176 | tf_op jit(solution)/shard_map/ppermute | solution.py:160
  36.9 1.2 %collective-permute-done.before = f32[64,8,128]{2,1,0:T(8,128)S(1)} collective-permute-done((f32[64,8,128]{2,1,0:T(8,128)S(1)}, f32[64,8,128]{2,1,0:T(8,128)S(1)}, u32[]{:S(2)}, u32[]{:S(2)}) %collective-permute-start) | collective-permute-done | bytes 262176 | tf_op jit(solution)/shard_map/ppermute | solution.py:159
  38.0 1.3 %collective-permute-start.2 = (f32[7,32,128]{2,1,0:T(8,128)S(1)}, f32[7,32,128]{2,1,0:T(8,128)S(1)}, u32[]{:S(2)}, u32[]{:S(2)}) collective-permute-start(f32[7,32,128]{2,1,0:T(8,128)S(1)} %pad_maximum_fusion), channel_id=1, source_target_pairs={{1,0},{2,1},{3,2},{4,3},{5,4},{6,5},{7,6},{9,8},{10,9},{11,10},{12... | collective-permute-start | bytes 344072 | tf_op jit(solution)/shard_map/ppermute | solution.py:163
  39.3 0.0 copy-done.2
  39.4 0.0 copy-done.3
  39.4 0.0 copy-done.4
  39.4 0.8 shard_map.64
  40.2 4.0 %collective-permute-done.2.edge = f32[7,32,128]{2,1,0:T(8,128)S(1)} collective-permute-done((f32[7,32,128]{2,1,0:T(8,128)S(1)}, f32[7,32,128]{2,1,0:T(8,128)S(1)}, u32[]{:S(2)}, u32[]{:S(2)}) %collective-permute-start.2) | collective-permute-done | bytes 114720 | tf_op jit(solution)/shard_map/ppermute | solution.py:163
  44.2 0.0 copy-done
  44.2 0.0 copy-done.1
  44.2 6.7 %shard_map.65 = (f32[4,4,128,256]{3,2,1,0:T(8,128)S(1)}, f32[128,128]{1,0:T(8,128)S(1)}) custom-call(f32[64,16,128]{2,1,0:T(8,128)S(1)} %bitcast.6, f32[64,8,128]{2,1,0:T(8,128)S(1)} %collective-permute-done.before, f32[64,8,128]{2,1,0:T(8,128)S(1)} %collective-permute-done.1.after, f32[7,32,128]{2,1,0:T(8,128)S(1)} %collective-permute-done.2.edge, ...), custom_call_target="tpu_custom_call" | custom-call | tf_op jit(solution)/shard_map/pallas_call | solution.py:164
  50.9 20.5 %all_to_all.29 = f32[64,2,128]{2,1,0:T(2,128)S(1)} all-to-all(f32[64,2,128]{2,1,0:T(2,128)S(1)} %bitcast.8), channel_id=1, replica_groups=mesh['tile'=64,'fblk'=8] {'tile'}, dimensions={0} | all-to-all | bytes 131072 | tf_op jit(solution)/shard_map/all_to_all | solution.py:175
  71.4 1.0 %shard_map.66 = f32[8,4,16,128]{3,2,1,0:T(8,128)S(1)} custom-call(s32[4]{0:T(128)S(1)} %copy-done.4, f32[128,128]{1,0:T(8,128)S(1)} %bitcast.7, f32[4,4,128,256]{3,2,1,0:T(8,128)S(1)} %get-tuple-element.12.refs_2_), custom_call_target="tpu_custom_call" | custom-call | tf_op jit(solution)/shard_map/pallas_call | solution.py:176
  72.4 20.4 %all_to_all.30 = f32[8,4,16,128]{3,2,1,0:T(8,128)S(1)} all-to-all(f32[8,4,16,128]{3,2,1,0:T(8,128)S(1)} %shard_map.66), channel_id=1, replica_groups=mesh['tile'=64,'fblk'=8] {'fblk'}, dimensions={0} | all-to-all | bytes 524288 | tf_op jit(solution)/shard_map/all_to_all | solution.py:184
  92.9 0.6 reduce_max.9
  (5 shorter events, 0.1 us)
Async XLA Ops:
  0.0 39.3 %copy-start.2 = (bf16[512,512]{1,0:T(8,128)(2,1)S(1)}, bf16[512,512]{1,0:T(8,128)(2,1)}, u32[]{:S(2)}) copy-start(bf16[512,512]{1,0:T(8,128)(2,1)} %constant.11.clone.low_in) | copy-start | bytes 1572868
  0.0 39.4 %copy-start.3 = (bf16[512,512]{1,0:T(8,128)(2,1)S(1)}, bf16[512,512]{1,0:T(8,128)(2,1)}, u32[]{:S(2)}) copy-start(bf16[512,512]{1,0:T(8,128)(2,1)} %constant.10.clone.high_in) | copy-start | bytes 1572868
  0.0 44.2 %copy-start = (bf16[4,256,256]{2,1,0:T(8,128)(2,1)S(1)}, bf16[4,256,256]{2,1,0:T(8,128)(2,1)}, u32[]{:S(2)}) copy-start(bf16[4,256,256]{2,1,0:T(8,128)(2,1)} %constant.13.clone.h_low) | copy-start | bytes 1572868
  0.0 44.2 %copy-start.1 = (bf16[4,256,256]{2,1,0:T(8,128)(2,1)S(1)}, bf16[4,256,256]{2,1,0:T(8,128)(2,1)}, u32[]{:S(2)}) copy-start(bf16[4,256,256]{2,1,0:T(8,128)(2,1)} %constant.12.clone.h_high) | copy-start | bytes 1572868
  0.0 39.3 %copy-start.4 = (s32[4]{0:T(128)S(1)}, s32[4]{0:T(128)}, u32[]{:S(2)}) copy-start(s32[4]{0:T(128)} %refs_0_.1) | copy-start | bytes 52
  29.2 7.7 %collective-permute-start.1 = (f32[64,8,128]{2,1,0:T(8,128)S(1)}, f32[64,8,128]{2,1,0:T(8,128)S(1)}, u32[]{:S(2)}, u32[]{:S(2)}) collective-permute-start(f32[64,8,128]{2,1,0:T(8,128)S(1)} %get-tuple-element.13), channel_id=1, source_target_pairs={{8,0},{16,8},{24,16},{32,24},{40,32},{48,40},{56,48},{64,56},{72,6... | collective-permute-start | bytes 786440 | tf_op jit(solution)/shard_map/ppermute | solution.py:160
  31.4 6.6 %collective-permute-start = (f32[64,8,128]{2,1,0:T(8,128)S(1)}, f32[64,8,128]{2,1,0:T(8,128)S(1)}, u32[]{:S(2)}, u32[]{:S(2)}) collective-permute-start(f32[64,8,128]{2,1,0:T(8,128)S(1)} %get-tuple-element.14), channel_id=1, source_target_pairs={{0,8},{8,16},{16,24},{24,32},{32,40},{40,48},{48,56},{56,64},{64,7... | collective-permute-start | bytes 786440 | tf_op jit(solution)/shard_map/ppermute | solution.py:159
  38.0 6.2 %collective-permute-start.2 = (f32[7,32,128]{2,1,0:T(8,128)S(1)}, f32[7,32,128]{2,1,0:T(8,128)S(1)}, u32[]{:S(2)}, u32[]{:S(2)}) collective-permute-start(f32[7,32,128]{2,1,0:T(8,128)S(1)} %pad_maximum_fusion), channel_id=1, source_target_pairs={{1,0},{2,1},{3,2},{4,3},{5,4},{6,5},{7,6},{9,8},{10,9},{11,10},{12... | collective-permute-start | bytes 344072 | tf_op jit(solution)/shard_map/ppermute | solution.py:163

commit v2 on v1

v2 whole, which is shorter than its diff:
```python
import jax
import jax.numpy as jnp
import numpy as np
from jax import lax
from jax.experimental import pallas as pl
from jax.experimental.pallas import tpu as pltpu
from jax.sharding import PartitionSpec as P

KERNELS = 4
RAD = 8
MAXW = 8
SIGMAS = (1.0, 1.6, 2.3, 3.2)
EPSILON = 1e-06
ROWS = 16
SPAN = ROWS + 2 * RAD
GROUP = 8
NX = 128
BLOCK = GROUP * ROWS
BF = jnp.bfloat16
F32 = jnp.float32
VMEM = pl.BlockSpec(memory_space=pltpu.VMEM)
SMEM = pl.BlockSpec(memory_space=pltpu.SMEM)
PARAMS = pltpu.CompilerParams(vmem_limit_bytes=32 * 1024 * 1024)


def taps(sigma):
    offsets = np.arange(2 * RAD + 1) - RAD
    values = np.exp(-(offsets**2) / (2.0 * sigma * sigma))
    return values / values.sum()


def split(matrix):
    matrix = np.asarray(matrix, np.float32)
    high = matrix.astype(BF)
    return high, (matrix - high.astype(np.float32)).astype(BF)


def vertical_matrix():
    out = np.zeros((KERNELS, GROUP, ROWS, 2 * GROUP, SPAN))
    for k, sigma in enumerate(SIGMAS):
        weights = taps(sigma)
        for row in range(ROWS):
            for channel in range(GROUP):
                for offset in range(MAXW):
                    out[k, channel, row, channel + offset, row : row + 2 * RAD + 1] = weights
    return out.reshape(KERNELS * GROUP * ROWS, 2 * GROUP * SPAN)


def horizontal_matrices():
    out = np.zeros((KERNELS, 2, NX, 2, NX))
    for k, sigma in enumerate(SIGMAS):
        weights = taps(sigma)
        for x in range(NX):
            for j in range(-RAD, RAD + 1):
                if 0 <= x + j < NX:
                    out[k, :, x + j, :, x] = weights[j + RAD] * np.eye(2)
    return out.reshape(KERNELS, 2 * NX, 2 * NX)


def halves(values):
    high = values.astype(BF)
    return high, (values - high.astype(F32)).astype(BF)


def dot(a, b):
    return jnp.dot(a, b, preferred_element_type=F32)


def dot3(a_high, a_low, b_high, b_low):
    return dot(a_high, b_high) + (dot(a_low, b_high) + dot(a_high, b_low))


def lane_sums(rows):
    return lax.dot_general(
        jnp.ones((8, NX), F32), rows, (((1,), (1,)), ((), ())), precision=lax.Precision.HIGHEST, preferred_element_type=F32
    )


def row_squares(values):
    return jnp.sum((values * values).reshape(GROUP, ROWS, values.shape[1]), axis=1)


def mask_kernel(widths, high_in, low_in, high, low):
    shape = (BLOCK, 2 * GROUP * SPAN)
    offset = lax.broadcasted_iota(jnp.int32, shape, 1) // SPAN - lax.broadcasted_iota(jnp.int32, shape, 0) // ROWS
    for k in range(KERNELS):
        keep = jnp.where(offset < widths[k], 1.0, 0.0)
        rows = pl.ds(k * BLOCK, BLOCK)
        high[rows, :] = (high_in[rows, :].astype(F32) * keep).astype(BF)
        low[rows, :] = (low_in[rows, :].astype(F32) * keep).astype(BF)


def framed(parity, own, flip, off):
    even = parity == 0
    return jnp.concatenate([jnp.where(even, off, flip), own, jnp.where(even, flip, off)], axis=1)


def main_kernel(parity, own, flip, off, a_high, a_low, h_high, h_low, smoothed, rest, sums, x_high, x_low, y_high, y_low):
    channels = own.shape[0]
    groups = channels // GROUP
    pairs = groups // 2
    x_high[0:channels], x_low[0:channels] = halves(framed(parity[0], own[...], flip[...], off[...]))
    x_high[channels:] = jnp.zeros((GROUP, SPAN, NX), BF)
    x_low[channels:] = jnp.zeros((GROUP, SPAN, NX), BF)
    for pair in range(pairs):

        def side_by_side(ref):
            first = 2 * pair * GROUP
            parts = [ref[first + s : first + s + 2 * GROUP].reshape(2 * GROUP * SPAN, NX) for s in (0, GROUP)]
            return jnp.concatenate(parts, axis=1)

        y = dot3(a_high[...], a_low[...], side_by_side(x_high), side_by_side(x_low))
        if pair == pairs - 1:
            rest[...] = y[:, NX:]
        yh, yl = halves(y)
        for k in range(KERNELS):
            y_high[k, pair * BLOCK : (pair + 1) * BLOCK] = yh[k * BLOCK : (k + 1) * BLOCK]
            y_low[k, pair * BLOCK : (pair + 1) * BLOCK] = yl[k * BLOCK : (k + 1) * BLOCK]
    squares = []
    for k in range(KERNELS):
        z = dot3(y_high[k], y_low[k], h_high[k], h_low[k])
        for pair in range(pairs):
            part = z[pair * BLOCK : (pair + 1) * BLOCK]
            smoothed[k, pair] = part
            squared = row_squares(part)
            squares += [squared[:, :NX], squared[:, NX:]][: groups - 1 - 2 * pair]
    squares.append(jnp.zeros((KERNELS * GROUP, NX), F32))
    sums[...] = lane_sums(jnp.concatenate(squares, axis=0))


def tail_kernel(parity, own, flip, off, a_high, a_low, h_high, h_low, rest, main_sums, smoothed, sums):
    x = framed(parity[0], own[...], flip[...], off[...])
    x = jnp.concatenate([x, jnp.zeros((1, SPAN, NX), F32)], axis=0)
    xh, xl = halves(x.reshape(GROUP * SPAN, NX))
    late = slice(GROUP * SPAN, 2 * GROUP * SPAN)
    yh, yl = halves(rest[...] + dot3(a_high[:, late], a_low[:, late], xh, xl))
    squares = [jnp.zeros((NX - KERNELS * GROUP, NX), F32)]
    for k in range(KERNELS):
        rows = slice(k * BLOCK, (k + 1) * BLOCK)
        z = dot3(yh[rows], yl[rows], h_high[k, :NX, :NX], h_low[k, :NX, :NX])
        smoothed[k] = z
        squares.append(row_squares(z))
    total = lane_sums(jnp.concatenate(squares, axis=0))
    low = jnp.broadcast_to(main_sums[0:1, :NX], sums.shape)
    high = jnp.broadcast_to(main_sums[0:1, NX:] + total[0:1], sums.shape)
    sums[...] = jnp.where(lax.broadcasted_iota(jnp.int32, sums.shape, 0) % 2 == 0, low, high)


def peak_kernel(cells, copies, widths, received, smoothed, last, peaks, scale):
    groups = 2 * smoothed.shape[1]
    per_kernel = (groups - 1) * GROUP
    row_odd = lax.broadcasted_iota(jnp.int32, (received.shape[0], NX), 0) % 2
    for h in (0, 1):
        scale[h * NX : (h + 1) * NX, :] = lax.dot_general(
            received[...],
            jnp.where(row_odd == h, 1.0, 0.0),
            (((0,), (0,)), ((), ())),
            precision=lax.Precision.HIGHEST,
            preferred_element_type=F32,
        )
    for k in range(KERNELS):
        floor = widths[k].astype(F32) * EPSILON
        spans = ((k * per_kernel, per_kernel), (KERNELS * per_kernel + k * GROUP, GROUP))
        inverse = [1.0 / jnp.sqrt(scale[at : at + size, :] * (1.0 / cells) + floor) for at, size in spans]
        best = None
        for group in range(groups):
            for c in range(GROUP):
                rows = slice(c * ROWS, (c + 1) * ROWS)
                if group < groups - 1:
                    lanes = slice((group % 2) * NX, (group % 2 + 1) * NX)
                    value = smoothed[k, group // 2, rows, lanes] * inverse[0][group * GROUP + c : group * GROUP + c + 1]
                else:
                    value = last[k, rows] * inverse[1][c : c + 1]
                best = value if best is None else jnp.maximum(best, value)
        for i in range(copies):
            peaks[i, k] = best


def call(kernel, out_shape, in_specs, scratch=(), flops=0, moved=0):
    return pl.pallas_call(
        kernel,
        out_shape=out_shape,
        in_specs=in_specs,
        out_specs=jax.tree.map(lambda _: VMEM, out_shape),
        scratch_shapes=list(scratch),
        compiler_params=PARAMS,
        cost_estimate=pl.CostEstimate(flops=flops, bytes_accessed=moved, transcendentals=0),
    )


def body(planes, widths):
    tiles, blocks = lax.axis_size("tile"), lax.axis_size("fblk")
    shape = jax.ShapeDtypeStruct
    parity = jnp.reshape(lax.axis_index("tile") % 2, (1,)).astype(jnp.int32)
    own = lax.all_to_all(planes, "tile", split_axis=1, concat_axis=0, tiled=True)
    channels = own.shape[0]
    pairs = channels // (2 * GROUP)
    cells = ROWS * tiles * NX
    a_high, a_low = map(jnp.asarray, split(vertical_matrix()))
    h_high, h_low = map(jnp.asarray, split(horizontal_matrices()))
    a_shape = shape(a_high.shape, BF)
    a_high, a_low = call(mask_kernel, [a_shape, a_shape], [SMEM, VMEM, VMEM], moved=2**21)(widths, a_high, a_low)

    odd = parity[0] == 1
    top, bottom = own[:, :RAD], own[:, ROWS - RAD :]
    inner = [(i + 1, i + 2) for i in range(0, tiles - 2, 2)]
    off = lax.ppermute(jnp.where(odd, bottom, top), "tile", inner + [(b, a) for a, b in inner])
    flip = lax.ppermute(jnp.where(odd, top, bottom), "tile", [(i, i ^ 1) for i in range(tiles)])
    first = slice(0, MAXW - 1)
    edge = jnp.concatenate([flip[first], own[first], off[first]], axis=1)
    edge = lax.ppermute(edge, "fblk", [(i + 1, i) for i in range(blocks - 1)])

    matrices = (a_high, a_low, h_high, h_low)
    smoothed, rest, sums = call(
        main_kernel,
        [
            shape((KERNELS, pairs, BLOCK, 2 * NX), F32),
            shape((KERNELS * BLOCK, NX), F32),
            shape((8, KERNELS * channels), F32),
        ],
        [SMEM] + [VMEM] * 7,
        [pltpu.VMEM((channels + GROUP, SPAN, NX), BF)] * 2 + [pltpu.VMEM((KERNELS, pairs * BLOCK, 2 * NX), BF)] * 2,
        flops=2**32,
        moved=2**23,
    )(parity, own, flip, off, *matrices)
    last, sums = call(
        tail_kernel,
        [shape((KERNELS, BLOCK, NX), F32), shape((2 * tiles, NX), F32)],
        [SMEM] + [VMEM] * 9,
        flops=2**29,
        moved=2**20,
    )(parity, edge[:, RAD : RAD + ROWS], edge[:, :RAD], edge[:, RAD + ROWS :], *matrices, rest, sums)
    received = lax.all_to_all(sums, "tile", split_axis=0, concat_axis=0, tiled=True)
    peaks = call(
        lambda *refs: peak_kernel(cells, blocks, *refs),
        shape((blocks, KERNELS, ROWS, NX), F32),
        [SMEM] + [VMEM] * 3,
        [pltpu.VMEM((KERNELS * channels, NX), F32)],
        moved=2**22,
    )(widths, received, smoothed, last)
    peaks = lax.all_to_all(peaks, "fblk", split_axis=0, concat_axis=0, tiled=True)
    return jnp.max(peaks, axis=0)


def solution(mesh):
    placed = (P(("fblk", "tile"), None, None), P())
    return jax.shard_map(body, mesh=mesh, in_specs=placed, out_specs=P(None, "tile", None), check_vma=False)
```

time: 93.8 us -> 86.3 us (0.920)
  blocking collectives: 70 us -> 37.8 us
  waiting for transfers between devices: 7.3 us -> 23 us
  starting transfers between devices: 6.85 us -> 18.3 us
  Pallas kernels: 8.51 us -> 5.98 us
    all_to_all x1 -> x0, blocking collectives: 29.1 us -> none  [body(): lax.all_to_all(planes, 'tile', split_axis=1, concat_axis=0, tiled=True)]
    all_to_all x0 -> x1, waiting for transfers between devices: none -> 17.3 us  [body(): lax.all_to_all(planes, 'tile', split_axis=1, concat_axis=0, tiled=True)]
    all_to_all x0 -> x1, starting transfers between devices: none -> 11.8 us  [body(): lax.all_to_all(planes, 'tile', split_axis=1, concat_axis=0, tiled=True)]
    all_to_all x1, blocking collectives: 20.5 us -> 17.4 us  [body(): lax.all_to_all(sums, 'tile', split_axis=0, concat_axis=0, tiled=True)]
    pallas_call x3 -> x4, Pallas kernels: 8.51 us -> 5.98 us  [the longest x1 3.3 us: body(): call(main_kernel, [shape((KERNELS, pairs, BLOCK, 2 * NX), F32), shape((KE...]
    ppermute x1, waiting for transfers between devices: 4.03 us -> 1.56 us  [body(): edge = lax.ppermute(edge, 'fblk', [(i + 1, i) for i in range(blocks - 1)])]
  transfers between devices with their start and end apart: 3 -> 4, of which waited for: 3 -> 3; matrix products, arithmetic and copies ran while one was open for 0% -> 0% of each run, Pallas kernels for 1% -> 5%
where the time goes in v2:
time: 86.3 us; the launch traced here: 85.9 us
  blocking collectives  37.8 us (44%)
  waiting for transfers between devices  23 us (27%)
  starting transfers between devices  18.3 us (21%)
  Pallas kernels  5.98 us (7%)
    all_to_all x1, blocking collectives, body(): lax.all_to_all(peaks, 'fblk', split_axis=0, concat_axis=0, tiled=True)  20.4 us
    all_to_all x1, blocking collectives, body(): lax.all_to_all(sums, 'tile', split_axis=0, concat_axis=0, tiled=True)  17.4 us
    all_to_all x1, waiting for transfers between devices, body(): lax.all_to_all(planes, 'tile', split_axis=1, concat_axis=0, tiled=True)  17.3 us
    all_to_all x1, starting transfers between devices, body(): lax.all_to_all(planes, 'tile', split_axis=1, concat_axis=0, tiled=True)  11.8 us
    ppermute x1, waiting for transfers between devices, body(): lax.ppermute(jnp.where(odd, bottom, top), 'tile', inner + [(b, a) for a,...  4.08 us
    pallas_call x1, Pallas kernels, body(): call(main_kernel, [shape((KERNELS, pairs, BLOCK, 2 * NX), F32), shape((KE...  3.3 us
    ppermute x1, starting transfers between devices, body(): lax.ppermute(jnp.where(odd, bottom, top), 'tile', inner + [(b, a) for a,...  3.01 us
    ppermute x1, starting transfers between devices, body(): lax.ppermute(jnp.where(odd, top, bottom), 'tile', [(i, i ^ 1) for i in ra...  2.23 us
  transfers between devices with their start and end apart: 4, of which 3 were waited for; matrix products, arithmetic and copies ran while one was open for 0% of the time, Pallas kernels for 5%

profile of v2, /device:TPU:1, one launch (start us, length us, event | category | flops | bytes accessed | tf_op | source)
XLA Modules:
  0.0 85.9 jit_solution(8117419353242378089)
XLA Ops:
  0.0 0.0 copy-start
  0.0 0.0 copy-start.1
  0.0 0.0 copy-start.2
  0.0 0.0 copy-start.3
  0.0 0.0 copy-start.4
  0.0 11.8 %all-to-all-start = ((f32[1,1024,128]{2,0,1:T(1,128)}), f32[1,1024,128]{2,0,1:T(1,128)S(1)}, u32[]{:S(2)}, u32[]{:S(2)}) async-start(f32[1,1024,128]{2,0,1:T(1,128)} %bitcast.10), calls=%async_computation | async-start | bytes 1048576 | tf_op jit(solution)/shard_map/all_to_all | solution.py:195
  11.8 17.3 %all-to-all-done = f32[1,1024,128]{2,0,1:T(1,128)S(1)} async-done(((f32[1,1024,128]{2,0,1:T(1,128)}), f32[1,1024,128]{2,0,1:T(1,128)S(1)}, u32[]{:S(2)}, u32[]{:S(2)}) %all-to-all-start) | async-done | bytes 524320 | tf_op jit(solution)/shard_map/all_to_all | solution.py:195
  29.2 2.2 %collective-permute-start = (f32[64,8,128]{2,1,0:T(8,128)S(1)}, f32[64,8,128]{2,1,0:T(8,128)S(1)}, u32[]{:S(2)}, u32[]{:S(2)}) collective-permute-start(f32[64,8,128]{2,1,0:T(8,128)S(1)} %get-tuple-element.19), channel_id=1, source_target_pairs={{0,8},{8,0},{16,24},{24,16},{32,40},{40,32},{48,56},{56,48},{64,72... | collective-permute-start | bytes 786440 | tf_op jit(solution)/shard_map/ppermute | solution.py:208
  31.4 3.0 %collective-permute-start.1 = (f32[64,8,128]{2,1,0:T(8,128)S(1)}, f32[64,8,128]{2,1,0:T(8,128)S(1)}, u32[]{:S(2)}, u32[]{:S(2)}) collective-permute-start(f32[64,8,128]{2,1,0:T(8,128)S(1)} %get-tuple-element.20), channel_id=1, source_target_pairs={{8,16},{24,32},{40,48},{56,64},{72,80},{88,96},{104,112},{120,128}... | collective-permute-start | bytes 786440 | tf_op jit(solution)/shard_map/ppermute | solution.py:207
  34.4 0.0 copy-done
  34.4 0.0 copy-done.1
  34.4 0.0 copy-done.4
  34.5 0.8 shard_map.64
  35.3 0.0 collective-permute-done.flip
  35.3 4.1 %collective-permute-done.1.off = f32[64,8,128]{2,1,0:T(8,128)S(1)} collective-permute-done((f32[64,8,128]{2,1,0:T(8,128)S(1)}, f32[64,8,128]{2,1,0:T(8,128)S(1)}, u32[]{:S(2)}, u32[]{:S(2)}) %collective-permute-start.1) | collective-permute-done | bytes 262176 | tf_op jit(solution)/shard_map/ppermute | solution.py:207
  39.4 1.3 %collective-permute-start.2 = (f32[7,32,128]{2,1,0:T(8,128)S(1)}, f32[7,32,128]{2,1,0:T(8,128)S(1)}, u32[]{:S(2)}, u32[]{:S(2)}) collective-permute-start(f32[7,32,128]{2,1,0:T(8,128)S(1)} %pad_maximum_fusion), channel_id=1, source_target_pairs={{1,0},{2,1},{3,2},{4,3},{5,4},{6,5},{7,6},{9,8},{10,9},{11,10},{12... | collective-permute-start | bytes 344072 | tf_op jit(solution)/shard_map/ppermute | solution.py:211
  40.7 0.0 copy-done.2
  40.7 0.0 copy-done.3
  40.7 3.3 %shard_map.65 = (f32[4,4,128,256]{3,2,1,0:T(8,128)S(1)}, f32[512,128]{1,0:T(8,128)S(1)}, f32[8,256]{1,0:T(8,128)S(1)}) custom-call(s32[1]{0:T(128)} %bitcast.parity, f32[64,16,128]{2,1,0:T(8,128)S(1)} %bitcast.7, f32[64,8,128]{2,1,0:T(8,128)S(1)} %collective-permute-done.flip, f32[64,8,128]{2,1,0:T(8,128)S(1)} %collective-permute-done.1.off, ...), custom_call_target="tpu_custom_call" | custom-call | flops 4294967296 | bytes 8388608 | tf_op jit(solution)/shard_map/pallas_call | solution.py:214
  44.0 1.6 %collective-permute-done.2 = f32[7,32,128]{2,1,0:T(8,128)S(1)} collective-permute-done((f32[7,32,128]{2,1,0:T(8,128)S(1)}, f32[7,32,128]{2,1,0:T(8,128)S(1)}, u32[]{:S(2)}, u32[]{:S(2)}) %collective-permute-start.2) | collective-permute-done | bytes 114720 | tf_op jit(solution)/shard_map/ppermute | solution.py:211
  45.6 0.8 shard_map.66
  46.4 17.4 %all_to_all.28 = f32[64,2,128]{2,1,0:T(2,128)S(1)} all-to-all(f32[64,2,128]{2,1,0:T(2,128)S(1)} %bitcast.9), channel_id=1, replica_groups=mesh['tile'=64,'fblk'=8] {'tile'}, dimensions={0} | all-to-all | bytes 131072 | tf_op jit(solution)/shard_map/all_to_all | solution.py:233
  63.8 1.1 %shard_map.67 = f32[8,4,16,128]{3,2,1,0:T(8,128)S(1)} custom-call(s32[4]{0:T(128)S(1)} %copy-done.4, f32[128,128]{1,0:T(8,128)S(1)} %bitcast.8, f32[4,4,128,256]{3,2,1,0:T(8,128)S(1)} %get-tuple-element.17.refs_2_, f32[4,128,128]{2,1,0:T(8,128)S(1)} %get-tuple-element.18.refs_3_), custom_call_target="tpu_custom_call" | custom-call | bytes 4194304 | tf_op jit(solution)/shard_map/pallas_call | solution.py:234
  64.9 20.4 %all_to_all.29 = f32[8,4,16,128]{3,2,1,0:T(8,128)S(1)} all-to-all(f32[8,4,16,128]{3,2,1,0:T(8,128)S(1)} %shard_map.67), channel_id=1, replica_groups=mesh['tile'=64,'fblk'=8] {'fblk'}, dimensions={0} | all-to-all | bytes 524288 | tf_op jit(solution)/shard_map/all_to_all | solution.py:241
  85.3 0.6 reduce_max.9
  (7 shorter events, 0.1 us)
Async XLA Ops:
  0.0 34.4 %copy-start = (bf16[512,512]{1,0:T(8,128)(2,1)S(1)}, bf16[512,512]{1,0:T(8,128)(2,1)}, u32[]{:S(2)}) copy-start(bf16[512,512]{1,0:T(8,128)(2,1)} %constant.30.clone.high_in) | copy-start | bytes 1572868
  0.0 34.4 %copy-start.1 = (bf16[512,512]{1,0:T(8,128)(2,1)S(1)}, bf16[512,512]{1,0:T(8,128)(2,1)}, u32[]{:S(2)}) copy-start(bf16[512,512]{1,0:T(8,128)(2,1)} %constant.31.clone.low_in) | copy-start | bytes 1572868
  0.0 40.7 %copy-start.2 = (bf16[4,256,256]{2,1,0:T(8,128)(2,1)S(1)}, bf16[4,256,256]{2,1,0:T(8,128)(2,1)}, u32[]{:S(2)}) copy-start(bf16[4,256,256]{2,1,0:T(8,128)(2,1)} %constant.32.clone.h_high) | copy-start | bytes 1572868
  0.0 40.7 %copy-start.3 = (bf16[4,256,256]{2,1,0:T(8,128)(2,1)S(1)}, bf16[4,256,256]{2,1,0:T(8,128)(2,1)}, u32[]{:S(2)}) copy-start(bf16[4,256,256]{2,1,0:T(8,128)(2,1)} %constant.33.clone.h_low) | copy-start | bytes 1572868
  0.0 34.4 %copy-start.4 = (s32[4]{0:T(128)S(1)}, s32[4]{0:T(128)}, u32[]{:S(2)}) copy-start(s32[4]{0:T(128)} %refs_0_.1) | copy-start | bytes 52
  0.0 29.1 %all-to-all-start = ((f32[1,1024,128]{2,0,1:T(1,128)}), f32[1,1024,128]{2,0,1:T(1,128)S(1)}, u32[]{:S(2)}, u32[]{:S(2)}) async-start(f32[1,1024,128]{2,0,1:T(1,128)} %bitcast.10), calls=%async_computation | async-start | bytes 1048576 | tf_op jit(solution)/shard_map/all_to_all | solution.py:195
  29.2 6.1 %collective-permute-start = (f32[64,8,128]{2,1,0:T(8,128)S(1)}, f32[64,8,128]{2,1,0:T(8,128)S(1)}, u32[]{:S(2)}, u32[]{:S(2)}) collective-permute-start(f32[64,8,128]{2,1,0:T(8,128)S(1)} %get-tuple-element.19), channel_id=1, source_target_pairs={{0,8},{8,0},{16,24},{24,16},{32,40},{40,32},{48,56},{56,48},{64,72... | collective-permute-start | bytes 786440 | tf_op jit(solution)/shard_map/ppermute | solution.py:208
  31.4 8.0 %collective-permute-start.1 = (f32[64,8,128]{2,1,0:T(8,128)S(1)}, f32[64,8,128]{2,1,0:T(8,128)S(1)}, u32[]{:S(2)}, u32[]{:S(2)}) collective-permute-start(f32[64,8,128]{2,1,0:T(8,128)S(1)} %get-tuple-element.20), channel_id=1, source_target_pairs={{8,16},{24,32},{40,48},{56,64},{72,80},{88,96},{104,112},{120,128}... | collective-permute-start | bytes 786440 | tf_op jit(solution)/shard_map/ppermute | solution.py:207
  39.4 6.2 %collective-permute-start.2 = (f32[7,32,128]{2,1,0:T(8,128)S(1)}, f32[7,32,128]{2,1,0:T(8,128)S(1)}, u32[]{:S(2)}, u32[]{:S(2)}) collective-permute-start(f32[7,32,128]{2,1,0:T(8,128)S(1)} %pad_maximum_fusion), channel_id=1, source_target_pairs={{1,0},{2,1},{3,2},{4,3},{5,4},{6,5},{7,6},{9,8},{10,9},{11,10},{12... | collective-permute-start | bytes 344072 | tf_op jit(solution)/shard_map/ppermute | solution.py:211

commit v3 on v2

--- a/solution.py
+++ b/solution.py
@@ -90,16 +90,16 @@
         low[rows, :] = (low_in[rows, :].astype(F32) * keep).astype(BF)
 
 
-def framed(parity, own, flip, off):
+def framed(parity, own, off, flip):
     even = parity == 0
     return jnp.concatenate([jnp.where(even, off, flip), own, jnp.where(even, flip, off)], axis=1)
 
 
-def main_kernel(parity, own, flip, off, a_high, a_low, h_high, h_low, smoothed, rest, sums, x_high, x_low, y_high, y_low):
+def main_kernel(parity, own, off, flip, a_high, a_low, h_high, h_low, smoothed, rest, sums, x_high, x_low, y_high, y_low):
     channels = own.shape[0]
     groups = channels // GROUP
     pairs = groups // 2
-    x_high[0:channels], x_low[0:channels] = halves(framed(parity[0], own[...], flip[...], off[...]))
+    x_high[0:channels], x_low[0:channels] = halves(framed(parity[0], own[...], off[...], flip[...]))
     x_high[channels:] = jnp.zeros((GROUP, SPAN, NX), BF)
     x_low[channels:] = jnp.zeros((GROUP, SPAN, NX), BF)
     for pair in range(pairs):
@@ -128,8 +128,8 @@
     sums[...] = lane_sums(jnp.concatenate(squares, axis=0))
 
 
-def tail_kernel(parity, own, flip, off, a_high, a_low, h_high, h_low, rest, main_sums, smoothed, sums):
-    x = framed(parity[0], own[...], flip[...], off[...])
+def tail_kernel(parity, own, off, flip, a_high, a_low, h_high, h_low, rest, main_sums, smoothed, sums):
+    x = framed(parity[0], own[...], off[...], flip[...])
     x = jnp.concatenate([x, jnp.zeros((1, SPAN, NX), F32)], axis=0)
     xh, xl = halves(x.reshape(GROUP * SPAN, NX))
     late = slice(GROUP * SPAN, 2 * GROUP * SPAN)
@@ -207,7 +207,7 @@
     off = lax.ppermute(jnp.where(odd, bottom, top), "tile", inner + [(b, a) for a, b in inner])
     flip = lax.ppermute(jnp.where(odd, top, bottom), "tile", [(i, i ^ 1) for i in range(tiles)])
     first = slice(0, MAXW - 1)
-    edge = jnp.concatenate([flip[first], own[first], off[first]], axis=1)
+    edge = jnp.concatenate([off[first], own[first], flip[first]], axis=1)
     edge = lax.ppermute(edge, "fblk", [(i + 1, i) for i in range(blocks - 1)])
 
     matrices = (a_high, a_low, h_high, h_low)
@@ -222,7 +222,7 @@
         [pltpu.VMEM((channels + GROUP, SPAN, NX), BF)] * 2 + [pltpu.VMEM((KERNELS, pairs * BLOCK, 2 * NX), BF)] * 2,
         flops=2**32,
         moved=2**23,
-    )(parity, own, flip, off, *matrices)
+    )(parity, own, off, flip, *matrices)
     last, sums = call(
         tail_kernel,
         [shape((KERNELS, BLOCK, NX), F32), shape((2 * tiles, NX), F32)],

time: 86.3 us -> 84.2 us (0.976)
  waiting for transfers between devices: 23 us -> 21 us
    ppermute x1, waiting for transfers between devices: 4.08 us -> 1.57 us  [body(): lax.ppermute(jnp.where(odd, bottom, top), 'tile', inner + [(b, a) for a,...]
where the time goes in v3:
time: 84.2 us; the launch traced here: 83.9 us
  blocking collectives  37.7 us (45%)
  waiting for transfers between devices  21 us (25%)
  starting transfers between devices  18.3 us (22%)
  Pallas kernels  5.98 us (7%)
    all_to_all x1, blocking collectives, body(): lax.all_to_all(peaks, 'fblk', split_axis=0, concat_axis=0, tiled=True)  20.4 us
    all_to_all x1, blocking collectives, body(): lax.all_to_all(sums, 'tile', split_axis=0, concat_axis=0, tiled=True)  17.3 us
    all_to_all x1, waiting for transfers between devices, body(): lax.all_to_all(planes, 'tile', split_axis=1, concat_axis=0, tiled=True)  17.3 us
    all_to_all x1, starting transfers between devices, body(): lax.all_to_all(planes, 'tile', split_axis=1, concat_axis=0, tiled=True)  11.8 us
    ppermute x1, starting transfers between devices, body(): lax.ppermute(jnp.where(odd, bottom, top), 'tile', inner + [(b, a) for a,...  3.32 us
    pallas_call x1, Pallas kernels, body(): call(main_kernel, [shape((KERNELS, pairs, BLOCK, 2 * NX), F32), shape((KE...  3.3 us
    ppermute x1, waiting for transfers between devices, body(): edge = lax.ppermute(edge, 'fblk', [(i + 1, i) for i in range(blocks - 1)])  2.15 us
    ppermute x1, starting transfers between devices, body(): lax.ppermute(jnp.where(odd, top, bottom), 'tile', [(i, i ^ 1) for i in ra...  1.92 us
  transfers between devices with their start and end apart: 4, of which 3 were waited for; matrix products, arithmetic and copies ran while one was open for 0% of the time, Pallas kernels for 5%

profile of v3, /device:TPU:1, one launch (start us, length us, event | category | flops | bytes accessed | tf_op | source)
XLA Modules:
  0.0 83.9 jit_solution(13039539102473602398)
XLA Ops:
  0.0 0.0 copy-start
  0.0 0.0 copy-start.1
  0.0 0.0 copy-start.2
  0.0 0.0 copy-start.3
  0.0 0.0 copy-start.4
  0.0 11.8 %all-to-all-start = ((f32[1,1024,128]{2,0,1:T(1,128)}), f32[1,1024,128]{2,0,1:T(1,128)S(1)}, u32[]{:S(2)}, u32[]{:S(2)}) async-start(f32[1,1024,128]{2,0,1:T(1,128)} %bitcast.10), calls=%async_computation | async-start | bytes 1048576 | tf_op jit(solution)/shard_map/all_to_all | solution.py:195
  11.8 17.3 %all-to-all-done = f32[1,1024,128]{2,0,1:T(1,128)S(1)} async-done(((f32[1,1024,128]{2,0,1:T(1,128)}), f32[1,1024,128]{2,0,1:T(1,128)S(1)}, u32[]{:S(2)}, u32[]{:S(2)}) %all-to-all-start) | async-done | bytes 524320 | tf_op jit(solution)/shard_map/all_to_all | solution.py:195
  29.2 3.3 %collective-permute-start = (f32[64,8,128]{2,1,0:T(8,128)S(1)}, f32[64,8,128]{2,1,0:T(8,128)S(1)}, u32[]{:S(2)}, u32[]{:S(2)}) collective-permute-start(f32[64,8,128]{2,1,0:T(8,128)S(1)} %get-tuple-element.19), channel_id=1, source_target_pairs={{8,16},{24,32},{40,48},{56,64},{72,80},{88,96},{104,112},{120,128}... | collective-permute-start | bytes 786440 | tf_op jit(solution)/shard_map/ppermute | solution.py:207
  32.5 1.9 %collective-permute-start.1 = (f32[64,8,128]{2,1,0:T(8,128)S(1)}, f32[64,8,128]{2,1,0:T(8,128)S(1)}, u32[]{:S(2)}, u32[]{:S(2)}) collective-permute-start(f32[64,8,128]{2,1,0:T(8,128)S(1)} %get-tuple-element.20), channel_id=1, source_target_pairs={{0,8},{8,0},{16,24},{24,16},{32,40},{40,32},{48,56},{56,48},{64,72... | collective-permute-start | bytes 786440 | tf_op jit(solution)/shard_map/ppermute | solution.py:208
  34.4 0.0 copy-done
  34.4 0.0 copy-done.1
  34.4 0.0 copy-done.4
  34.5 0.8 shard_map.64
  35.3 1.6 %collective-permute-done.off = f32[64,8,128]{2,1,0:T(8,128)S(1)} collective-permute-done((f32[64,8,128]{2,1,0:T(8,128)S(1)}, f32[64,8,128]{2,1,0:T(8,128)S(1)}, u32[]{:S(2)}, u32[]{:S(2)}) %collective-permute-start) | collective-permute-done | bytes 262176 | tf_op jit(solution)/shard_map/ppermute | solution.py:207
  36.9 0.0 collective-permute-done.1.flip
  36.9 1.3 %collective-permute-start.2 = (f32[7,32,128]{2,1,0:T(8,128)S(1)}, f32[7,32,128]{2,1,0:T(8,128)S(1)}, u32[]{:S(2)}, u32[]{:S(2)}) collective-permute-start(f32[7,32,128]{2,1,0:T(8,128)S(1)} %pad_maximum_fusion), channel_id=1, source_target_pairs={{1,0},{2,1},{3,2},{4,3},{5,4},{6,5},{7,6},{9,8},{10,9},{11,10},{12... | collective-permute-start | bytes 344072 | tf_op jit(solution)/shard_map/ppermute | solution.py:211
  38.2 0.0 copy-done.2
  38.2 0.0 copy-done.3
  38.2 3.3 %shard_map.65 = (f32[4,4,128,256]{3,2,1,0:T(8,128)S(1)}, f32[512,128]{1,0:T(8,128)S(1)}, f32[8,256]{1,0:T(8,128)S(1)}) custom-call(s32[1]{0:T(128)} %bitcast.parity, f32[64,16,128]{2,1,0:T(8,128)S(1)} %bitcast.7, f32[64,8,128]{2,1,0:T(8,128)S(1)} %collective-permute-done.off, f32[64,8,128]{2,1,0:T(8,128)S(1)} %collective-permute-done.1.flip, ...), custom_call_target="tpu_custom_call" | custom-call | flops 4294967296 | bytes 8388608 | tf_op jit(solution)/shard_map/pallas_call | solution.py:214
  41.5 2.2 %collective-permute-done.2 = f32[7,32,128]{2,1,0:T(8,128)S(1)} collective-permute-done((f32[7,32,128]{2,1,0:T(8,128)S(1)}, f32[7,32,128]{2,1,0:T(8,128)S(1)}, u32[]{:S(2)}, u32[]{:S(2)}) %collective-permute-start.2) | collective-permute-done | bytes 114720 | tf_op jit(solution)/shard_map/ppermute | solution.py:211
  43.7 0.8 shard_map.66
  44.5 17.3 %all_to_all.28 = f32[64,2,128]{2,1,0:T(2,128)S(1)} all-to-all(f32[64,2,128]{2,1,0:T(2,128)S(1)} %bitcast.9), channel_id=1, replica_groups=mesh['tile'=64,'fblk'=8] {'tile'}, dimensions={0} | all-to-all | bytes 131072 | tf_op jit(solution)/shard_map/all_to_all | solution.py:233
  61.8 1.1 %shard_map.67 = f32[8,4,16,128]{3,2,1,0:T(8,128)S(1)} custom-call(s32[4]{0:T(128)S(1)} %copy-done.4, f32[128,128]{1,0:T(8,128)S(1)} %bitcast.8, f32[4,4,128,256]{3,2,1,0:T(8,128)S(1)} %get-tuple-element.17.refs_2_, f32[4,128,128]{2,1,0:T(8,128)S(1)} %get-tuple-element.18.refs_3_), custom_call_target="tpu_custom_call" | custom-call | bytes 4194304 | tf_op jit(solution)/shard_map/pallas_call | solution.py:234
  62.9 20.4 %all_to_all.29 = f32[8,4,16,128]{3,2,1,0:T(8,128)S(1)} all-to-all(f32[8,4,16,128]{3,2,1,0:T(8,128)S(1)} %shard_map.67), channel_id=1, replica_groups=mesh['tile'=64,'fblk'=8] {'fblk'}, dimensions={0} | all-to-all | bytes 524288 | tf_op jit(solution)/shard_map/all_to_all | solution.py:241
  83.3 0.6 reduce_max.9
  (7 shorter events, 0.1 us)
Async XLA Ops:
  0.0 34.4 %copy-start = (bf16[512,512]{1,0:T(8,128)(2,1)S(1)}, bf16[512,512]{1,0:T(8,128)(2,1)}, u32[]{:S(2)}) copy-start(bf16[512,512]{1,0:T(8,128)(2,1)} %constant.30.clone.high_in) | copy-start | bytes 1572868
  0.0 34.4 %copy-start.1 = (bf16[512,512]{1,0:T(8,128)(2,1)S(1)}, bf16[512,512]{1,0:T(8,128)(2,1)}, u32[]{:S(2)}) copy-start(bf16[512,512]{1,0:T(8,128)(2,1)} %constant.31.clone.low_in) | copy-start | bytes 1572868
  0.0 38.2 %copy-start.2 = (bf16[4,256,256]{2,1,0:T(8,128)(2,1)S(1)}, bf16[4,256,256]{2,1,0:T(8,128)(2,1)}, u32[]{:S(2)}) copy-start(bf16[4,256,256]{2,1,0:T(8,128)(2,1)} %constant.32.clone.h_high) | copy-start | bytes 1572868
  0.0 38.2 %copy-start.3 = (bf16[4,256,256]{2,1,0:T(8,128)(2,1)S(1)}, bf16[4,256,256]{2,1,0:T(8,128)(2,1)}, u32[]{:S(2)}) copy-start(bf16[4,256,256]{2,1,0:T(8,128)(2,1)} %constant.33.clone.h_low) | copy-start | bytes 1572868
  0.0 34.4 %copy-start.4 = (s32[4]{0:T(128)S(1)}, s32[4]{0:T(128)}, u32[]{:S(2)}) copy-start(s32[4]{0:T(128)} %refs_0_.1) | copy-start | bytes 52
  0.0 29.1 %all-to-all-start = ((f32[1,1024,128]{2,0,1:T(1,128)}), f32[1,1024,128]{2,0,1:T(1,128)S(1)}, u32[]{:S(2)}, u32[]{:S(2)}) async-start(f32[1,1024,128]{2,0,1:T(1,128)} %bitcast.10), calls=%async_computation | async-start | bytes 1048576 | tf_op jit(solution)/shard_map/all_to_all | solution.py:195
  29.2 7.7 %collective-permute-start = (f32[64,8,128]{2,1,0:T(8,128)S(1)}, f32[64,8,128]{2,1,0:T(8,128)S(1)}, u32[]{:S(2)}, u32[]{:S(2)}) collective-permute-start(f32[64,8,128]{2,1,0:T(8,128)S(1)} %get-tuple-element.19), channel_id=1, source_target_pairs={{8,16},{24,32},{40,48},{56,64},{72,80},{88,96},{104,112},{120,128}... | collective-permute-start | bytes 786440 | tf_op jit(solution)/shard_map/ppermute | solution.py:207
  32.5 4.4 %collective-permute-start.1 = (f32[64,8,128]{2,1,0:T(8,128)S(1)}, f32[64,8,128]{2,1,0:T(8,128)S(1)}, u32[]{:S(2)}, u32[]{:S(2)}) collective-permute-start(f32[64,8,128]{2,1,0:T(8,128)S(1)} %get-tuple-element.20), channel_id=1, source_target_pairs={{0,8},{8,0},{16,24},{24,16},{32,40},{40,32},{48,56},{56,48},{64,72... | collective-permute-start | bytes 786440 | tf_op jit(solution)/shard_map/ppermute | solution.py:208
  36.9 6.8 %collective-permute-start.2 = (f32[7,32,128]{2,1,0:T(8,128)S(1)}, f32[7,32,128]{2,1,0:T(8,128)S(1)}, u32[]{:S(2)}, u32[]{:S(2)}) collective-permute-start(f32[7,32,128]{2,1,0:T(8,128)S(1)} %pad_maximum_fusion), channel_id=1, source_target_pairs={{1,0},{2,1},{3,2},{4,3},{5,4},{6,5},{7,6},{9,8},{10,9},{11,10},{12... | collective-permute-start | bytes 344072 | tf_op jit(solution)/shard_map/ppermute | solution.py:211

commit v4 on v3

--- a/solution.py
+++ b/solution.py
@@ -200,6 +200,7 @@
     h_high, h_low = map(jnp.asarray, split(horizontal_matrices()))
     a_shape = shape(a_high.shape, BF)
     a_high, a_low = call(mask_kernel, [a_shape, a_shape], [SMEM, VMEM, VMEM], moved=2**21)(widths, a_high, a_low)
+    own, a_high, a_low = lax.optimization_barrier((own, a_high, a_low))
 
     odd = parity[0] == 1
     top, bottom = own[:, :RAD], own[:, ROWS - RAD :]
@@ -230,7 +231,9 @@
         flops=2**29,
         moved=2**20,
     )(parity, edge[:, RAD : RAD + ROWS], edge[:, :RAD], edge[:, RAD + ROWS :], *matrices, rest, sums)
-    received = lax.all_to_all(sums, "tile", split_axis=0, concat_axis=0, tiled=True)
+    received = lax.all_to_all(
+        sums, "tile", split_axis=0, concat_axis=0, tiled=True, axis_index_groups=[list(range(tiles))[::-1]]
+    )
     peaks = call(
         lambda *refs: peak_kernel(cells, blocks, *refs),
         shape((blocks, KERNELS, ROWS, NX), F32),
@@ -238,7 +241,9 @@
         [pltpu.VMEM((KERNELS * channels, NX), F32)],
         moved=2**22,
     )(widths, received, smoothed, last)
-    peaks = lax.all_to_all(peaks, "fblk", split_axis=0, concat_axis=0, tiled=True)
+    peaks = lax.all_to_all(
+        peaks, "fblk", split_axis=0, concat_axis=0, tiled=True, axis_index_groups=[list(range(blocks))[::-1]]
+    )
     return jnp.max(peaks, axis=0)
 
 

time: 84.2 us -> 79.5 us (0.944)
  the two profiles are of different devices: /device:TPU:1 before, /device:TPU:64 now
where the time goes in v4:
time: 79.5 us; the launch traced here: 79.1 us
  blocking collectives  34.3 us (43%)
  starting transfers between devices  18 us (23%)
  waiting for transfers between devices  17.3 us (22%)
  Pallas kernels  5.86 us (7%)
  local copies, waits for them, and re-layouts  2.77 us (3%)
    all_to_all x1, blocking collectives, body(): lax.all_to_all(peaks, 'fblk', split_axis=0, concat_axis=0, tiled=True, ax...  18.3 us
    all_to_all x1, blocking collectives, body(): lax.all_to_all(sums, 'tile', split_axis=0, concat_axis=0, tiled=True, axi...  16.1 us
    all_to_all x1, waiting for transfers between devices, body(): lax.all_to_all(planes, 'tile', split_axis=1, concat_axis=0, tiled=True)  13.6 us
    all_to_all x1, starting transfers between devices, body(): lax.all_to_all(planes, 'tile', split_axis=1, concat_axis=0, tiled=True)  10.7 us
    ppermute x1, starting transfers between devices, body(): lax.ppermute(jnp.where(odd, top, bottom), 'tile', [(i, i ^ 1) for i in ra...  4.74 us
    pallas_call x1, Pallas kernels, body(): call(main_kernel, [shape((KERNELS, pairs, BLOCK, 2 * NX), F32), shape((KE...  3.19 us
    unnamed x12, local copies, waits for them, and re-layouts  2.74 us
    ppermute x1, waiting for transfers between devices, body(): edge = lax.ppermute(edge, 'fblk', [(i + 1, i) for i in range(blocks - 1)])  2.55 us
  transfers between devices with their start and end apart: 4, of which 3 were waited for; matrix products, arithmetic and copies ran while one was open for 0% of the time, Pallas kernels for 5%

profile of v4, /device:TPU:64, one launch (start us, length us, event | category | flops | bytes accessed | tf_op | source)
XLA Modules:
  0.0 79.1 jit_solution(15824447354823959232)
XLA Ops:
  0.0 0.0 copy-start.2
  0.0 0.0 copy-start.3
  0.0 10.7 %all-to-all-start = ((f32[1,1024,128]{2,0,1:T(1,128)}), f32[1,1024,128]{2,0,1:T(1,128)S(1)}, u32[]{:S(2)}, u32[]{:S(2)}) async-start(f32[1,1024,128]{2,0,1:T(1,128)} %bitcast.10), calls=%async_computation | async-start | bytes 1048576 | tf_op jit(solution)/shard_map/all_to_all | solution.py:195
  10.7 0.0 copy-start
  10.7 1.0 %copy-done = bf16[512,512]{1,0:T(8,128)(2,1)S(1)} copy-done((bf16[512,512]{1,0:T(8,128)(2,1)S(1)}, bf16[512,512]{1,0:T(8,128)(2,1)}, u32[]{:S(2)}) %copy-start) | copy-done | bytes 524312
  11.8 0.0 copy-start.1
  11.8 1.0 %copy-done.1 = bf16[512,512]{1,0:T(8,128)(2,1)S(1)} copy-done((bf16[512,512]{1,0:T(8,128)(2,1)S(1)}, bf16[512,512]{1,0:T(8,128)(2,1)}, u32[]{:S(2)}) %copy-start.1) | copy-done | bytes 524312
  12.8 0.0 copy-start.4
  12.8 0.7 copy-done.4
  13.5 0.8 %shard_map.64 = (bf16[512,512]{1,0:T(8,128)(2,1)S(1)}, bf16[512,512]{1,0:T(8,128)(2,1)S(1)}) custom-call(s32[4]{0:T(128)S(1)} %copy-done.4, bf16[512,512]{1,0:T(8,128)(2,1)S(1)} %copy-done, bf16[512,512]{1,0:T(8,128)(2,1)S(1)} %copy-done.1), custom_call_target="tpu_custom_call" | custom-call | bytes 2097152 | tf_op jit(solution)/shard_map/pallas_call | solution.py:202
  14.3 13.6 %all-to-all-done = f32[1,1024,128]{2,0,1:T(1,128)S(1)} async-done(((f32[1,1024,128]{2,0,1:T(1,128)}), f32[1,1024,128]{2,0,1:T(1,128)S(1)}, u32[]{:S(2)}, u32[]{:S(2)}) %all-to-all-start) | async-done | bytes 524320 | tf_op jit(solution)/shard_map/all_to_all | solution.py:195
  27.9 0.7 collective-permute-start
  28.6 4.7 %collective-permute-start.1 = (f32[64,8,128]{2,1,0:T(8,128)S(1)}, f32[64,8,128]{2,1,0:T(8,128)S(1)}, u32[]{:S(2)}, u32[]{:S(2)}) collective-permute-start(f32[64,8,128]{2,1,0:T(8,128)S(1)} %get-tuple-element.26), channel_id=1, source_target_pairs={{0,8},{8,0},{16,24},{24,16},{32,40},{40,32},{48,56},{56,48},{64,72... | collective-permute-start | bytes 786440 | tf_op jit(solution)/shard_map/ppermute | solution.py:209
  33.4 0.0 collective-permute-done.off
  33.4 1.1 %collective-permute-done.1.flip = f32[64,8,128]{2,1,0:T(8,128)S(1)} collective-permute-done((f32[64,8,128]{2,1,0:T(8,128)S(1)}, f32[64,8,128]{2,1,0:T(8,128)S(1)}, u32[]{:S(2)}, u32[]{:S(2)}) %collective-permute-start.1) | collective-permute-done | bytes 262176 | tf_op jit(solution)/shard_map/ppermute | solution.py:209
  34.5 1.9 %collective-permute-start.2 = (f32[7,32,128]{2,1,0:T(8,128)S(1)}, f32[7,32,128]{2,1,0:T(8,128)S(1)}, u32[]{:S(2)}, u32[]{:S(2)}) collective-permute-start(f32[7,32,128]{2,1,0:T(8,128)S(1)} %pad_maximum_fusion), channel_id=1, source_target_pairs={{1,0},{2,1},{3,2},{4,3},{5,4},{6,5},{7,6},{9,8},{10,9},{11,10},{12... | collective-permute-start | bytes 344072 | tf_op jit(solution)/shard_map/ppermute | solution.py:212
  36.5 0.0 copy-done.2
  36.5 0.0 copy-done.3
  36.5 3.2 %shard_map.65 = (f32[4,4,128,256]{3,2,1,0:T(8,128)S(1)}, f32[512,128]{1,0:T(8,128)S(1)}, f32[8,256]{1,0:T(8,128)S(1)}) custom-call(s32[1]{0:T(128)} %bitcast.parity, f32[64,16,128]{2,1,0:T(8,128)S(1)} %bitcast.7, f32[64,8,128]{2,1,0:T(8,128)S(1)} %collective-permute-done.off, f32[64,8,128]{2,1,0:T(8,128)S(1)} %collective-permute-done.1.flip, ...), custom_call_target="tpu_custom_call" | custom-call | flops 4294967296 | bytes 8388608 | tf_op jit(solution)/shard_map/pallas_call | solution.py:215
  39.7 0.0 copy-start.5
  39.7 2.5 %collective-permute-done.2 = f32[7,32,128]{2,1,0:T(8,128)S(1)} collective-permute-done((f32[7,32,128]{2,1,0:T(8,128)S(1)}, f32[7,32,128]{2,1,0:T(8,128)S(1)}, u32[]{:S(2)}, u32[]{:S(2)}) %collective-permute-start.2) | collective-permute-done | bytes 114720 | tf_op jit(solution)/shard_map/ppermute | solution.py:212
  42.2 0.8 %shard_map.66 = (f32[4,128,128]{2,1,0:T(8,128)S(1)}, f32[128,128]{1,0:T(8,128)S(1)}) custom-call(s32[1]{0:T(128)} %bitcast.parity, f32[7,16,128]{2,1,0:T(8,128)S(1)} %slice.34.own, f32[7,8,128]{2,1,0:T(8,128)S(1)} %get-tuple-element.28.off, f32[7,8,128]{2,1,0:T(8,128)S(1)} %get-tuple-element.27.flip, bf16[512,512]{1,0:T(8,128)(2,1)S(1)} %get-tuple-element.18.a_high, ...), custom_call_target="tpu_custom_call" | custom-call | flops 536870912 | bytes 1048576 | tf_op jit(solution)/shard_map/pallas_call | solution.py:227
  43.0 16.1 %all_to_all.28 = f32[64,2,128]{2,1,0:T(2,128)S(1)} all-to-all(f32[64,2,128]{2,1,0:T(2,128)S(1)} %bitcast.9), channel_id=1, replica_groups={{504,496,488,480,472,464,456,448,440,432,424,416,408,400,392,384,376,36..., dimensions={0} | all-to-all | bytes 131072 | tf_op jit(solution)/shard_map/all_to_all | solution.py:234
  59.1 0.0 copy-done.5
  59.1 1.1 %shard_map.67 = f32[8,4,16,128]{3,2,1,0:T(8,128)S(1)} custom-call(s32[4]{0:T(128)S(1)} %copy-done.5, f32[128,128]{1,0:T(8,128)S(1)} %bitcast.8, f32[4,4,128,256]{3,2,1,0:T(8,128)S(1)} %get-tuple-element.23.refs_2_, f32[4,128,128]{2,1,0:T(8,128)S(1)} %get-tuple-element.24.refs_3_), custom_call_target="tpu_custom_call" | custom-call | bytes 4194304 | tf_op jit(solution)/shard_map/pallas_call | solution.py:237
  60.2 18.3 %all_to_all.29 = f32[8,4,16,128]{3,2,1,0:T(8,128)S(1)} all-to-all(f32[8,4,16,128]{3,2,1,0:T(8,128)S(1)} %shard_map.67), channel_id=1, replica_groups={{7,6,5,4,3,2,1,0},{15,14,13,12,11,10,9,8},{23,22,21,20,19,18,17,16},{31..., dimensions={0} | all-to-all | bytes 524288 | tf_op jit(solution)/shard_map/all_to_all | solution.py:244
  78.4 0.6 reduce_max.9
  (7 shorter events, 0.1 us)
Async XLA Ops:
  0.0 36.5 %copy-start.2 = (bf16[4,256,256]{2,1,0:T(8,128)(2,1)S(1)}, bf16[4,256,256]{2,1,0:T(8,128)(2,1)}, u32[]{:S(2)}) copy-start(bf16[4,256,256]{2,1,0:T(8,128)(2,1)} %constant.32.clone.h_high) | copy-start | bytes 1572868
  0.0 36.5 %copy-start.3 = (bf16[4,256,256]{2,1,0:T(8,128)(2,1)S(1)}, bf16[4,256,256]{2,1,0:T(8,128)(2,1)}, u32[]{:S(2)}) copy-start(bf16[4,256,256]{2,1,0:T(8,128)(2,1)} %constant.33.clone.h_low) | copy-start | bytes 1572868
  0.0 27.9 %all-to-all-start = ((f32[1,1024,128]{2,0,1:T(1,128)}), f32[1,1024,128]{2,0,1:T(1,128)S(1)}, u32[]{:S(2)}, u32[]{:S(2)}) async-start(f32[1,1024,128]{2,0,1:T(1,128)} %bitcast.10), calls=%async_computation | async-start | bytes 1048576 | tf_op jit(solution)/shard_map/all_to_all | solution.py:195
  10.7 1.0 %copy-start = (bf16[512,512]{1,0:T(8,128)(2,1)S(1)}, bf16[512,512]{1,0:T(8,128)(2,1)}, u32[]{:S(2)}) copy-start(bf16[512,512]{1,0:T(8,128)(2,1)} %constant.30.clone.high_in) | copy-start | bytes 1572868
  11.8 1.0 %copy-start.1 = (bf16[512,512]{1,0:T(8,128)(2,1)S(1)}, bf16[512,512]{1,0:T(8,128)(2,1)}, u32[]{:S(2)}) copy-start(bf16[512,512]{1,0:T(8,128)(2,1)} %constant.31.clone.low_in) | copy-start | bytes 1572868
  12.8 0.7 copy-start.4
  27.9 5.4 %collective-permute-start = (f32[64,8,128]{2,1,0:T(8,128)S(1)}, f32[64,8,128]{2,1,0:T(8,128)S(1)}, u32[]{:S(2)}, u32[]{:S(2)}) collective-permute-start(f32[64,8,128]{2,1,0:T(8,128)S(1)} %get-tuple-element.25), channel_id=1, source_target_pairs={{8,16},{24,32},{40,48},{56,64},{72,80},{88,96},{104,112},{120,128}... | collective-permute-start | bytes 786440 | tf_op jit(solution)/shard_map/ppermute | solution.py:208
  28.6 5.9 %collective-permute-start.1 = (f32[64,8,128]{2,1,0:T(8,128)S(1)}, f32[64,8,128]{2,1,0:T(8,128)S(1)}, u32[]{:S(2)}, u32[]{:S(2)}) collective-permute-start(f32[64,8,128]{2,1,0:T(8,128)S(1)} %get-tuple-element.26), channel_id=1, source_target_pairs={{0,8},{8,0},{16,24},{24,16},{32,40},{40,32},{48,56},{56,48},{64,72... | collective-permute-start | bytes 786440 | tf_op jit(solution)/shard_map/ppermute | solution.py:209
  34.5 7.7 %collective-permute-start.2 = (f32[7,32,128]{2,1,0:T(8,128)S(1)}, f32[7,32,128]{2,1,0:T(8,128)S(1)}, u32[]{:S(2)}, u32[]{:S(2)}) collective-permute-start(f32[7,32,128]{2,1,0:T(8,128)S(1)} %pad_maximum_fusion), channel_id=1, source_target_pairs={{1,0},{2,1},{3,2},{4,3},{5,4},{6,5},{7,6},{9,8},{10,9},{11,10},{12... | collective-permute-start | bytes 344072 | tf_op jit(solution)/shard_map/ppermute | solution.py:212
  39.7 19.4 %copy-start.5 = (s32[4]{0:T(128)S(1)}, s32[4]{0:T(128)}, u32[]{:S(2)}) copy-start(s32[4]{0:T(128)} %refs_0_.1) | copy-start | bytes 52

commit v5 on v4

--- a/solution.py
+++ b/solution.py
@@ -12,10 +12,10 @@
 SIGMAS = (1.0, 1.6, 2.3, 3.2)
 EPSILON = 1e-06
 ROWS = 16
-SPAN = ROWS + 2 * RAD
 GROUP = 8
 NX = 128
 BLOCK = GROUP * ROWS
+DEPTH = 2 * GROUP * ROWS
 BF = jnp.bfloat16
 F32 = jnp.float32
 VMEM = pl.BlockSpec(memory_space=pltpu.VMEM)
@@ -36,14 +36,16 @@
 
 
 def vertical_matrix():
-    out = np.zeros((KERNELS, GROUP, ROWS, 2 * GROUP, SPAN))
+    out = np.zeros((KERNELS, GROUP, ROWS, 2 * GROUP, ROWS + 2 * RAD))
     for k, sigma in enumerate(SIGMAS):
         weights = taps(sigma)
         for row in range(ROWS):
             for channel in range(GROUP):
                 for offset in range(MAXW):
                     out[k, channel, row, channel + offset, row : row + 2 * RAD + 1] = weights
-    return out.reshape(KERNELS * GROUP * ROWS, 2 * GROUP * SPAN)
+    own = out[..., RAD : RAD + ROWS]
+    border = np.concatenate([out[..., :RAD], out[..., RAD + ROWS :]], axis=-1)
+    return np.concatenate([x.reshape(KERNELS * BLOCK, DEPTH) for x in (own, border)], axis=1)
 
 
 def horizontal_matrices():
@@ -71,9 +73,11 @@
 
 
 def lane_sums(rows):
-    return lax.dot_general(
-        jnp.ones((8, NX), F32), rows, (((1,), (1,)), ((), ())), precision=lax.Precision.HIGHEST, preferred_element_type=F32
-    )
+    ones = jnp.ones((8, NX), BF)
+    parts = [
+        lax.dot_general(ones, half, (((1,), (1,)), ((), ())), preferred_element_type=F32) for half in halves(rows)
+    ]
+    return parts[0] + parts[1]
 
 
 def row_squares(values):
@@ -81,8 +85,9 @@
 
 
 def mask_kernel(widths, high_in, low_in, high, low):
-    shape = (BLOCK, 2 * GROUP * SPAN)
-    offset = lax.broadcasted_iota(jnp.int32, shape, 1) // SPAN - lax.broadcasted_iota(jnp.int32, shape, 0) // ROWS
+    shape = (BLOCK, 2 * DEPTH)
+    column = lax.broadcasted_iota(jnp.int32, shape, 1) % DEPTH
+    offset = column // ROWS - lax.broadcasted_iota(jnp.int32, shape, 0) // ROWS
     for k in range(KERNELS):
         keep = jnp.where(offset < widths[k], 1.0, 0.0)
         rows = pl.ds(k * BLOCK, BLOCK)
@@ -90,26 +95,38 @@
         low[rows, :] = (low_in[rows, :].astype(F32) * keep).astype(BF)
 
 
-def framed(parity, own, off, flip):
+def border_rows(parity, off, flip):
     even = parity == 0
-    return jnp.concatenate([jnp.where(even, off, flip), own, jnp.where(even, flip, off)], axis=1)
-
-
-def main_kernel(parity, own, off, flip, a_high, a_low, h_high, h_low, smoothed, rest, sums, x_high, x_low, y_high, y_low):
-    channels = own.shape[0]
-    groups = channels // GROUP
-    pairs = groups // 2
-    x_high[0:channels], x_low[0:channels] = halves(framed(parity[0], own[...], off[...], flip[...]))
-    x_high[channels:] = jnp.zeros((GROUP, SPAN, NX), BF)
-    x_low[channels:] = jnp.zeros((GROUP, SPAN, NX), BF)
+    return jnp.concatenate([jnp.where(even, off, flip), jnp.where(even, flip, off)], axis=1)
+
+
+def fill(values, high, low):
+    channels = values.shape[0]
+    high[0:channels], low[0:channels] = halves(values)
+    high[channels:] = jnp.zeros((GROUP, ROWS, NX), BF)
+    low[channels:] = jnp.zeros((GROUP, ROWS, NX), BF)
+
+
+def side_by_side(ref, pair):
+    first = 2 * pair * GROUP
+    parts = [ref[first + s : first + s + 2 * GROUP].reshape(DEPTH, NX) for s in (0, GROUP)]
+    return jnp.concatenate(parts, axis=1)
+
+
+def own_kernel(own, a_high, a_low, partial, x_high, x_low):
+    fill(own[...], x_high, x_low)
+    for pair in range(partial.shape[0]):
+        xs = side_by_side(x_high, pair), side_by_side(x_low, pair)
+        partial[pair] = dot3(a_high[:, :DEPTH], a_low[:, :DEPTH], *xs)
+
+
+def main_kernel(parity, off, flip, partial, a_high, a_low, h_high, h_low, smoothed, rest, sums, x_high, x_low, y_high, y_low):
+    pairs = partial.shape[0]
+    groups = 2 * pairs
+    fill(border_rows(parity[0], off[...], flip[...]), x_high, x_low)
     for pair in range(pairs):
-
-        def side_by_side(ref):
-            first = 2 * pair * GROUP
-            parts = [ref[first + s : first + s + 2 * GROUP].reshape(2 * GROUP * SPAN, NX) for s in (0, GROUP)]
-            return jnp.concatenate(parts, axis=1)
-
-        y = dot3(a_high[...], a_low[...], side_by_side(x_high), side_by_side(x_low))
+        xs = side_by_side(x_high, pair), side_by_side(x_low, pair)
+        y = partial[pair] + dot3(a_high[:, DEPTH:], a_low[:, DEPTH:], *xs)
         if pair == pairs - 1:
             rest[...] = y[:, NX:]
         yh, yl = halves(y)
@@ -128,12 +145,13 @@
     sums[...] = lane_sums(jnp.concatenate(squares, axis=0))
 
 
-def tail_kernel(parity, own, off, flip, a_high, a_low, h_high, h_low, rest, main_sums, smoothed, sums):
-    x = framed(parity[0], own[...], off[...], flip[...])
-    x = jnp.concatenate([x, jnp.zeros((1, SPAN, NX), F32)], axis=0)
-    xh, xl = halves(x.reshape(GROUP * SPAN, NX))
-    late = slice(GROUP * SPAN, 2 * GROUP * SPAN)
-    yh, yl = halves(rest[...] + dot3(a_high[:, late], a_low[:, late], xh, xl))
+def tail_kernel(parity, edge, a_high, a_low, h_high, h_low, rest, main_sums, smoothed, sums):
+    values = jnp.concatenate([edge[...], jnp.zeros((1, ROWS + 2 * RAD, NX), F32)], axis=0)
+    border = border_rows(parity[0], values[:, :RAD], values[:, RAD + ROWS :])
+    x = [part.reshape(BLOCK, NX) for part in (values[:, RAD : RAD + ROWS], border)]
+    late = [slice(BLOCK, DEPTH), slice(DEPTH + BLOCK, 2 * DEPTH)]
+    a = [jnp.concatenate([ref[:, part] for part in late], axis=1) for ref in (a_high, a_low)]
+    yh, yl = halves(rest[...] + dot3(*a, *halves(jnp.concatenate(x, axis=0))))
     squares = [jnp.zeros((NX - KERNELS * GROUP, NX), F32)]
     for k in range(KERNELS):
         rows = slice(k * BLOCK, (k + 1) * BLOCK)
@@ -149,28 +167,29 @@
 def peak_kernel(cells, copies, widths, received, smoothed, last, peaks, scale):
     groups = 2 * smoothed.shape[1]
     per_kernel = (groups - 1) * GROUP
-    row_odd = lax.broadcasted_iota(jnp.int32, (received.shape[0], NX), 0) % 2
+    total = jnp.sum(received[...].reshape(-1, 8, NX), axis=0)
+    total = total[0:2] + total[2:4] + (total[4:6] + total[6:8])
     for h in (0, 1):
-        scale[h * NX : (h + 1) * NX, :] = lax.dot_general(
-            received[...],
-            jnp.where(row_odd == h, 1.0, 0.0),
-            (((0,), (0,)), ((), ())),
-            precision=lax.Precision.HIGHEST,
-            preferred_element_type=F32,
-        )
-    for k in range(KERNELS):
-        floor = widths[k].astype(F32) * EPSILON
-        spans = ((k * per_kernel, per_kernel), (KERNELS * per_kernel + k * GROUP, GROUP))
-        inverse = [1.0 / jnp.sqrt(scale[at : at + size, :] * (1.0 / cells) + floor) for at, size in spans]
+        index = h * NX + lax.broadcasted_iota(jnp.int32, (1, NX), 1)
+        kernel = jnp.where(index < KERNELS * per_kernel, index // per_kernel, (index - KERNELS * per_kernel) // GROUP)
+        width = jnp.full((1, NX), widths[0], jnp.int32)
+        for k in range(1, KERNELS):
+            width = jnp.where(kernel == k, widths[k], width)
+        inverse = 1.0 / jnp.sqrt(total[h : h + 1] * (1.0 / cells) + width.astype(F32) * EPSILON)
+        scale[h * NX : (h + 1) * NX, :] = jnp.broadcast_to(inverse, (NX, NX)).T
+    for k in range(KERNELS):
         best = None
         for group in range(groups):
             for c in range(GROUP):
                 rows = slice(c * ROWS, (c + 1) * ROWS)
                 if group < groups - 1:
                     lanes = slice((group % 2) * NX, (group % 2 + 1) * NX)
-                    value = smoothed[k, group // 2, rows, lanes] * inverse[0][group * GROUP + c : group * GROUP + c + 1]
+                    at = k * per_kernel + group * GROUP + c
+                    value = smoothed[k, group // 2, rows, lanes]
                 else:
-                    value = last[k, rows] * inverse[1][c : c + 1]
+                    at = KERNELS * per_kernel + k * GROUP + c
+                    value = last[k, rows]
+                value = value * scale[at : at + 1]
                 best = value if best is None else jnp.maximum(best, value)
         for i in range(copies):
             peaks[i, k] = best
@@ -212,6 +231,15 @@
     edge = lax.ppermute(edge, "fblk", [(i + 1, i) for i in range(blocks - 1)])
 
     matrices = (a_high, a_low, h_high, h_low)
+    rows_scratch = [pltpu.VMEM((channels + GROUP, ROWS, NX), BF)] * 2
+    partial = call(
+        own_kernel,
+        shape((pairs, KERNELS * BLOCK, 2 * NX), F32),
+        [VMEM] * 3,
+        rows_scratch,
+        flops=2**30,
+        moved=2**22,
+    )(own, a_high, a_low)
     smoothed, rest, sums = call(
         main_kernel,
         [
@@ -220,17 +248,17 @@
             shape((8, KERNELS * channels), F32),
         ],
         [SMEM] + [VMEM] * 7,
-        [pltpu.VMEM((channels + GROUP, SPAN, NX), BF)] * 2 + [pltpu.VMEM((KERNELS, pairs * BLOCK, 2 * NX), BF)] * 2,
-        flops=2**32,
+        rows_scratch + [pltpu.VMEM((KERNELS, pairs * BLOCK, 2 * NX), BF)] * 2,
+        flops=2**31,
         moved=2**23,
-    )(parity, own, off, flip, *matrices)
+    )(parity, off, flip, partial, *matrices)
     last, sums = call(
         tail_kernel,
         [shape((KERNELS, BLOCK, NX), F32), shape((2 * tiles, NX), F32)],
-        [SMEM] + [VMEM] * 9,
+        [SMEM] + [VMEM] * 7,
         flops=2**29,
         moved=2**20,
-    )(parity, edge[:, RAD : RAD + ROWS], edge[:, :RAD], edge[:, RAD + ROWS :], *matrices, rest, sums)
+    )(parity, edge, *matrices, rest, sums)
     received = lax.all_to_all(
         sums, "tile", split_axis=0, concat_axis=0, tiled=True, axis_index_groups=[list(range(tiles))[::-1]]
     )

time: 79.5 us -> 79 us (level)
    ppermute x1, waiting for transfers between devices: 2.55 us -> 3.74 us  [body(): edge = lax.ppermute(edge, 'fblk', [(i + 1, i) for i in range(blocks - 1)])]
    pallas_call x1, Pallas kernels: 3.19 us -> 2 us  [body(): call(main_kernel, [shape((KERNELS, pairs, BLOCK, 2 * NX), F32), shape((KE...]
    ppermute x1, waiting for transfers between devices: 1.1 us -> 0.05 us  [body(): lax.ppermute(jnp.where(odd, top, bottom), 'tile', [(i, i ^ 1) for i in ra...]
    pallas_call x0 -> x1, Pallas kernels: none -> 1.03 us  [body(): call(own_kernel, shape((pairs, KERNELS * BLOCK, 2 * NX), F32), [VMEM] * 3...]
  transfers between devices with their start and end apart: 4 -> 4, of which waited for: 3 -> 2; matrix products, arithmetic and copies ran while one was open for 0% -> 0% of each run, Pallas kernels for 5% -> 5%
where the time goes in v5:
time: 79 us; the launch traced here: 78.6 us
  blocking collectives  34.3 us (43%)
  starting transfers between devices  17.9 us (23%)
  waiting for transfers between devices  17.4 us (22%)
  Pallas kernels  5.36 us (7%)
  local copies, waits for them, and re-layouts  2.76 us (3%)
    all_to_all x1, blocking collectives, body(): lax.all_to_all(peaks, 'fblk', split_axis=0, concat_axis=0, tiled=True, ax...  18.3 us
    all_to_all x1, blocking collectives, body(): lax.all_to_all(sums, 'tile', split_axis=0, concat_axis=0, tiled=True, axi...  16 us
    all_to_all x1, waiting for transfers between devices, body(): lax.all_to_all(planes, 'tile', split_axis=1, concat_axis=0, tiled=True)  13.6 us
    all_to_all x1, starting transfers between devices, body(): lax.all_to_all(planes, 'tile', split_axis=1, concat_axis=0, tiled=True)  10.6 us
    ppermute x1, starting transfers between devices, body(): lax.ppermute(jnp.where(odd, top, bottom), 'tile', [(i, i ^ 1) for i in ra...  4.74 us
    ppermute x1, waiting for transfers between devices, body(): edge = lax.ppermute(edge, 'fblk', [(i + 1, i) for i in range(blocks - 1)])  3.74 us
    unnamed x12, local copies, waits for them, and re-layouts  2.75 us
    pallas_call x1, Pallas kernels, body(): call(main_kernel, [shape((KERNELS, pairs, BLOCK, 2 * NX), F32), shape((KE...  2 us
  transfers between devices with their start and end apart: 4, of which 2 were waited for; matrix products, arithmetic and copies ran while one was open for 0% of the time, Pallas kernels for 5%

profile of v5, /device:TPU:64, one launch (start us, length us, event | category | flops | bytes accessed | tf_op | source)
XLA Modules:
  0.0 78.6 jit_solution(14667265712212250194)
XLA Ops:
  0.0 10.6 %all-to-all-start = ((f32[1,1024,128]{2,0,1:T(1,128)}), f32[1,1024,128]{2,0,1:T(1,128)S(1)}, u32[]{:S(2)}, u32[]{:S(2)}) async-start(f32[1,1024,128]{2,0,1:T(1,128)} %bitcast.10), calls=%async_computation | async-start | bytes 1048576 | tf_op jit(solution)/shard_map/all_to_all | solution.py:214
  10.6 0.0 copy-start
  10.6 1.0 %copy-done = bf16[512,512]{1,0:T(8,128)(2,1)S(1)} copy-done((bf16[512,512]{1,0:T(8,128)(2,1)S(1)}, bf16[512,512]{1,0:T(8,128)(2,1)}, u32[]{:S(2)}) %copy-start) | copy-done | bytes 524312
  11.6 0.0 copy-start.1
  11.6 1.0 %copy-done.1 = bf16[512,512]{1,0:T(8,128)(2,1)S(1)} copy-done((bf16[512,512]{1,0:T(8,128)(2,1)S(1)}, bf16[512,512]{1,0:T(8,128)(2,1)}, u32[]{:S(2)}) %copy-start.1) | copy-done | bytes 524312
  12.7 0.0 copy-start.4
  12.7 0.7 copy-done.4
  13.3 0.8 %shard_map.64 = (bf16[512,512]{1,0:T(8,128)(2,1)S(1)}, bf16[512,512]{1,0:T(8,128)(2,1)S(1)}) custom-call(s32[4]{0:T(128)S(1)} %copy-done.4, bf16[512,512]{1,0:T(8,128)(2,1)S(1)} %copy-done.1, bf16[512,512]{1,0:T(8,128)(2,1)S(1)} %copy-done), custom_call_target="tpu_custom_call" | custom-call | bytes 2097152 | tf_op jit(solution)/shard_map/pallas_call | solution.py:221
  14.1 13.6 %all-to-all-done = f32[1,1024,128]{2,0,1:T(1,128)S(1)} async-done(((f32[1,1024,128]{2,0,1:T(1,128)}), f32[1,1024,128]{2,0,1:T(1,128)S(1)}, u32[]{:S(2)}, u32[]{:S(2)}) %all-to-all-start) | async-done | bytes 524320 | tf_op jit(solution)/shard_map/all_to_all | solution.py:214
  27.8 0.7 collective-permute-start
  28.5 4.7 %collective-permute-start.1 = (f32[64,8,128]{2,1,0:T(8,128)S(1)}, f32[64,8,128]{2,1,0:T(8,128)S(1)}, u32[]{:S(2)}, u32[]{:S(2)}) collective-permute-start(f32[64,8,128]{2,1,0:T(8,128)S(1)} %get-tuple-element.26), channel_id=1, source_target_pairs={{0,8},{8,0},{16,24},{24,16},{32,40},{40,32},{48,56},{56,48},{64,72... | collective-permute-start | bytes 786440 | tf_op jit(solution)/shard_map/ppermute | solution.py:228
  33.3 0.0 copy-start.2
  33.3 0.0 copy-start.3
  33.3 1.0 %shard_map.65.partial = f32[4,512,256]{2,1,0:T(8,128)S(1)} custom-call(f32[64,16,128]{2,1,0:T(8,128)S(1)} %bitcast.7, bf16[512,512]{1,0:T(8,128)(2,1)S(1)} %get-tuple-element.18.a_high, bf16[512,512]{1,0:T(8,128)(2,1)S(1)} %get-tuple-element.19.a_low), custom_call_target="tpu_custom_call" | custom-call | flops 1073741824 | bytes 4194304 | tf_op jit(solution)/shard_map/pallas_call | solution.py:235
  34.3 0.0 collective-permute-done.off
  34.3 0.0 collective-permute-done.1.flip
  34.4 1.9 %collective-permute-start.2 = (f32[7,32,128]{2,1,0:T(8,128)S(1)}, f32[7,32,128]{2,1,0:T(8,128)S(1)}, u32[]{:S(2)}, u32[]{:S(2)}) collective-permute-start(f32[7,32,128]{2,1,0:T(8,128)S(1)} %pad_maximum_fusion), channel_id=1, source_target_pairs={{1,0},{2,1},{3,2},{4,3},{5,4},{6,5},{7,6},{9,8},{10,9},{11,10},{12... | collective-permute-start | bytes 344072 | tf_op jit(solution)/shard_map/ppermute | solution.py:231
  36.3 0.0 copy-done.2
  36.3 0.0 copy-done.3
  36.3 2.0 %shard_map.66 = (f32[4,4,128,256]{3,2,1,0:T(8,128)S(1)}, f32[512,128]{1,0:T(8,128)S(1)}, f32[8,256]{1,0:T(8,128)S(1)}) custom-call(s32[1]{0:T(128)} %bitcast.parity, f32[64,8,128]{2,1,0:T(8,128)S(1)} %collective-permute-done.off, f32[64,8,128]{2,1,0:T(8,128)S(1)} %collective-permute-done.1.flip, f32[4,512,256]{2,1,0:T(8,128)S(1)} %shard_map.65.partial, ...), custom_call_target="tpu_custom_call" | custom-call | flops 2147483648 | bytes 8388608 | tf_op jit(solution)/shard_map/pallas_call | solution.py:243
  38.3 0.0 copy-start.5
  38.4 3.7 %collective-permute-done.2.edge = f32[7,32,128]{2,1,0:T(8,128)S(1)} collective-permute-done((f32[7,32,128]{2,1,0:T(8,128)S(1)}, f32[7,32,128]{2,1,0:T(8,128)S(1)}, u32[]{:S(2)}, u32[]{:S(2)}) %collective-permute-start.2) | collective-permute-done | bytes 114720 | tf_op jit(solution)/shard_map/ppermute | solution.py:231
  42.1 0.7 shard_map.67
  42.8 16.0 %all_to_all.28 = f32[64,2,128]{2,1,0:T(2,128)S(1)} all-to-all(f32[64,2,128]{2,1,0:T(2,128)S(1)} %bitcast.9), channel_id=1, replica_groups={{504,496,488,480,472,464,456,448,440,432,424,416,408,400,392,384,376,36..., dimensions={0} | all-to-all | bytes 131072 | tf_op jit(solution)/shard_map/all_to_all | solution.py:262
  58.9 0.0 copy-done.5
  58.9 0.8 %shard_map.68 = f32[8,4,16,128]{3,2,1,0:T(8,128)S(1)} custom-call(s32[4]{0:T(128)S(1)} %copy-done.5, f32[128,128]{1,0:T(8,128)S(1)} %bitcast.8, f32[4,4,128,256]{3,2,1,0:T(8,128)S(1)} %get-tuple-element.23.refs_2_, f32[4,128,128]{2,1,0:T(8,128)S(1)} %get-tuple-element.24.refs_3_), custom_call_target="tpu_custom_call" | custom-call | bytes 4194304 | tf_op jit(solution)/shard_map/pallas_call | solution.py:265
  59.7 18.3 %all_to_all.29 = f32[8,4,16,128]{3,2,1,0:T(8,128)S(1)} all-to-all(f32[8,4,16,128]{3,2,1,0:T(8,128)S(1)} %shard_map.68), channel_id=1, replica_groups={{7,6,5,4,3,2,1,0},{15,14,13,12,11,10,9,8},{23,22,21,20,19,18,17,16},{31..., dimensions={0} | all-to-all | bytes 524288 | tf_op jit(solution)/shard_map/all_to_all | solution.py:272
  78.0 0.6 reduce_max.9
  (5 shorter events, 0.1 us)
Async XLA Ops:
  0.0 27.8 %all-to-all-start = ((f32[1,1024,128]{2,0,1:T(1,128)}), f32[1,1024,128]{2,0,1:T(1,128)S(1)}, u32[]{:S(2)}, u32[]{:S(2)}) async-start(f32[1,1024,128]{2,0,1:T(1,128)} %bitcast.10), calls=%async_computation | async-start | bytes 1048576 | tf_op jit(solution)/shard_map/all_to_all | solution.py:214
  10.6 1.0 %copy-start = (bf16[512,512]{1,0:T(8,128)(2,1)S(1)}, bf16[512,512]{1,0:T(8,128)(2,1)}, u32[]{:S(2)}) copy-start(bf16[512,512]{1,0:T(8,128)(2,1)} %constant.31.clone.low_in) | copy-start | bytes 1572868
  11.6 1.0 %copy-start.1 = (bf16[512,512]{1,0:T(8,128)(2,1)S(1)}, bf16[512,512]{1,0:T(8,128)(2,1)}, u32[]{:S(2)}) copy-start(bf16[512,512]{1,0:T(8,128)(2,1)} %constant.30.clone.high_in) | copy-start | bytes 1572868
  12.7 0.7 copy-start.4
  27.8 6.5 %collective-permute-start = (f32[64,8,128]{2,1,0:T(8,128)S(1)}, f32[64,8,128]{2,1,0:T(8,128)S(1)}, u32[]{:S(2)}, u32[]{:S(2)}) collective-permute-start(f32[64,8,128]{2,1,0:T(8,128)S(1)} %get-tuple-element.25), channel_id=1, source_target_pairs={{8,16},{24,32},{40,48},{56,64},{72,80},{88,96},{104,112},{120,128}... | collective-permute-start | bytes 786440 | tf_op jit(solution)/shard_map/ppermute | solution.py:227
  28.5 5.9 %collective-permute-start.1 = (f32[64,8,128]{2,1,0:T(8,128)S(1)}, f32[64,8,128]{2,1,0:T(8,128)S(1)}, u32[]{:S(2)}, u32[]{:S(2)}) collective-permute-start(f32[64,8,128]{2,1,0:T(8,128)S(1)} %get-tuple-element.26), channel_id=1, source_target_pairs={{0,8},{8,0},{16,24},{24,16},{32,40},{40,32},{48,56},{56,48},{64,72... | collective-permute-start | bytes 786440 | tf_op jit(solution)/shard_map/ppermute | solution.py:228
  33.3 3.1 %copy-start.2 = (bf16[4,256,256]{2,1,0:T(8,128)(2,1)S(1)}, bf16[4,256,256]{2,1,0:T(8,128)(2,1)}, u32[]{:S(2)}) copy-start(bf16[4,256,256]{2,1,0:T(8,128)(2,1)} %constant.33.clone.h_low) | copy-start | bytes 1572868
  33.3 3.1 %copy-start.3 = (bf16[4,256,256]{2,1,0:T(8,128)(2,1)S(1)}, bf16[4,256,256]{2,1,0:T(8,128)(2,1)}, u32[]{:S(2)}) copy-start(bf16[4,256,256]{2,1,0:T(8,128)(2,1)} %constant.32.clone.h_high) | copy-start | bytes 1572868
  34.4 7.7 %collective-permute-start.2 = (f32[7,32,128]{2,1,0:T(8,128)S(1)}, f32[7,32,128]{2,1,0:T(8,128)S(1)}, u32[]{:S(2)}, u32[]{:S(2)}) collective-permute-start(f32[7,32,128]{2,1,0:T(8,128)S(1)} %pad_maximum_fusion), channel_id=1, source_target_pairs={{1,0},{2,1},{3,2},{4,3},{5,4},{6,5},{7,6},{9,8},{10,9},{11,10},{12... | collective-permute-start | bytes 344072 | tf_op jit(solution)/shard_map/ppermute | solution.py:231
  38.3 20.5 %copy-start.5 = (s32[4]{0:T(128)S(1)}, s32[4]{0:T(128)}, u32[]{:S(2)}) copy-start(s32[4]{0:T(128)} %refs_0_.1) | copy-start | bytes 52

commit v6 on v5

--- a/solution.py
+++ b/solution.py
@@ -145,10 +145,10 @@
     sums[...] = lane_sums(jnp.concatenate(squares, axis=0))
 
 
-def tail_kernel(parity, edge, a_high, a_low, h_high, h_low, rest, main_sums, smoothed, sums):
-    values = jnp.concatenate([edge[...], jnp.zeros((1, ROWS + 2 * RAD, NX), F32)], axis=0)
-    border = border_rows(parity[0], values[:, :RAD], values[:, RAD + ROWS :])
-    x = [part.reshape(BLOCK, NX) for part in (values[:, RAD : RAD + ROWS], border)]
+def tail_kernel(parity, edge_own, edge, a_high, a_low, h_high, h_low, rest, main_sums, smoothed, sums):
+    border = border_rows(parity[0], edge[:, :RAD], edge[:, RAD:])
+    zero = jnp.zeros((1, ROWS, NX), F32)
+    x = [jnp.concatenate([part, zero], axis=0).reshape(BLOCK, NX) for part in (edge_own[...], border)]
     late = [slice(BLOCK, DEPTH), slice(DEPTH + BLOCK, 2 * DEPTH)]
     a = [jnp.concatenate([ref[:, part] for part in late], axis=1) for ref in (a_high, a_low)]
     yh, yl = halves(rest[...] + dot3(*a, *halves(jnp.concatenate(x, axis=0))))
@@ -227,8 +227,10 @@
     off = lax.ppermute(jnp.where(odd, bottom, top), "tile", inner + [(b, a) for a, b in inner])
     flip = lax.ppermute(jnp.where(odd, top, bottom), "tile", [(i, i ^ 1) for i in range(tiles)])
     first = slice(0, MAXW - 1)
-    edge = jnp.concatenate([off[first], own[first], flip[first]], axis=1)
-    edge = lax.ppermute(edge, "fblk", [(i + 1, i) for i in range(blocks - 1)])
+    previous = [(i + 1, i) for i in range(blocks - 1)]
+    edge_own = lax.ppermute(own[first], "fblk", previous)
+    edge = jnp.concatenate([off[first], flip[first]], axis=1)
+    edge = lax.ppermute(edge, "fblk", previous)
 
     matrices = (a_high, a_low, h_high, h_low)
     rows_scratch = [pltpu.VMEM((channels + GROUP, ROWS, NX), BF)] * 2
@@ -255,10 +257,10 @@
     last, sums = call(
         tail_kernel,
         [shape((KERNELS, BLOCK, NX), F32), shape((2 * tiles, NX), F32)],
-        [SMEM] + [VMEM] * 7,
+        [SMEM] + [VMEM] * 8,
         flops=2**29,
         moved=2**20,
-    )(parity, edge, *matrices, rest, sums)
+    )(parity, edge_own, edge, *matrices, rest, sums)
     received = lax.all_to_all(
         sums, "tile", split_axis=0, concat_axis=0, tiled=True, axis_index_groups=[list(range(tiles))[::-1]]
     )

time: 79 us -> 78.3 us (level)
  starting transfers between devices: 17.9 us -> 20 us
  blocking collectives: 34.3 us -> 32.7 us
  waiting for transfers between devices: 17.4 us -> 16.1 us
    ppermute x1 -> x2, starting transfers between devices: 1.92 us -> 3.97 us  [the longest x1 2.05 us: body(): edge_own = lax.ppermute(own[first], 'fblk', previous)]
    all_to_all x1, blocking collectives: 16 us -> 14.4 us  [body(): lax.all_to_all(sums, 'tile', split_axis=0, concat_axis=0, tiled=True, axi...]
    ppermute x1 -> x2, waiting for transfers between devices: 3.74 us -> 2.44 us  [the longest x1 2.42 us: body(): edge = lax.ppermute(edge, 'fblk', previous)]
  transfers between devices with their start and end apart: 4 -> 5, of which waited for: 2 -> 2; matrix products, arithmetic and copies ran while one was open for 0% -> 0% of each run, Pallas kernels for 5% -> 5%
where the time goes in v6:
time: 78.3 us; the launch traced here: 77.8 us
  blocking collectives  32.7 us (42%)
  starting transfers between devices  20 us (26%)
  waiting for transfers between devices  16.1 us (21%)
  Pallas kernels  5.43 us (7%)
  local copies, waits for them, and re-layouts  2.76 us (4%)
    all_to_all x1, blocking collectives, body(): lax.all_to_all(peaks, 'fblk', split_axis=0, concat_axis=0, tiled=True, ax...  18.3 us
    all_to_all x1, blocking collectives, body(): lax.all_to_all(sums, 'tile', split_axis=0, concat_axis=0, tiled=True, axi...  14.4 us
    all_to_all x1, waiting for transfers between devices, body(): lax.all_to_all(planes, 'tile', split_axis=1, concat_axis=0, tiled=True)  13.6 us
    all_to_all x1, starting transfers between devices, body(): lax.all_to_all(planes, 'tile', split_axis=1, concat_axis=0, tiled=True)  10.6 us
    ppermute x1, starting transfers between devices, body(): lax.ppermute(jnp.where(odd, top, bottom), 'tile', [(i, i ^ 1) for i in ra...  4.74 us
    unnamed x12, local copies, waits for them, and re-layouts  2.75 us
    ppermute x1, waiting for transfers between devices, body(): edge = lax.ppermute(edge, 'fblk', previous)  2.42 us
    ppermute x1, starting transfers between devices, body(): edge_own = lax.ppermute(own[first], 'fblk', previous)  2.05 us
  transfers between devices with their start and end apart: 5, of which 2 were waited for; matrix products, arithmetic and copies ran while one was open for 0% of the time, Pallas kernels for 5%

profile of v6, /device:TPU:64, one launch (start us, length us, event | category | flops | bytes accessed | tf_op | source)
XLA Modules:
  0.0 77.8 jit_solution(16170018158474677946)
XLA Ops:
  0.0 10.6 %all-to-all-start = ((f32[1,1024,128]{2,0,1:T(1,128)}), f32[1,1024,128]{2,0,1:T(1,128)S(1)}, u32[]{:S(2)}, u32[]{:S(2)}) async-start(f32[1,1024,128]{2,0,1:T(1,128)} %bitcast.10), calls=%async_computation | async-start | bytes 1048576 | tf_op jit(solution)/shard_map/all_to_all | solution.py:214
  10.6 0.0 copy-start
  10.6 1.0 %copy-done = bf16[512,512]{1,0:T(8,128)(2,1)S(1)} copy-done((bf16[512,512]{1,0:T(8,128)(2,1)S(1)}, bf16[512,512]{1,0:T(8,128)(2,1)}, u32[]{:S(2)}) %copy-start) | copy-done | bytes 524312
  11.6 0.0 copy-start.1
  11.6 1.0 %copy-done.1 = bf16[512,512]{1,0:T(8,128)(2,1)S(1)} copy-done((bf16[512,512]{1,0:T(8,128)(2,1)S(1)}, bf16[512,512]{1,0:T(8,128)(2,1)}, u32[]{:S(2)}) %copy-start.1) | copy-done | bytes 524312
  12.7 0.0 copy-start.4
  12.7 0.7 copy-done.4
  13.3 0.8 %shard_map.64 = (bf16[512,512]{1,0:T(8,128)(2,1)S(1)}, bf16[512,512]{1,0:T(8,128)(2,1)S(1)}) custom-call(s32[4]{0:T(128)S(1)} %copy-done.4, bf16[512,512]{1,0:T(8,128)(2,1)S(1)} %copy-done.1, bf16[512,512]{1,0:T(8,128)(2,1)S(1)} %copy-done), custom_call_target="tpu_custom_call" | custom-call | bytes 2097152 | tf_op jit(solution)/shard_map/pallas_call | solution.py:221
  14.1 13.6 %all-to-all-done = f32[1,1024,128]{2,0,1:T(1,128)S(1)} async-done(((f32[1,1024,128]{2,0,1:T(1,128)}), f32[1,1024,128]{2,0,1:T(1,128)S(1)}, u32[]{:S(2)}, u32[]{:S(2)}) %all-to-all-start) | async-done | bytes 524320 | tf_op jit(solution)/shard_map/all_to_all | solution.py:214
  27.8 0.7 collective-permute-start.1
  28.5 4.7 %collective-permute-start.2 = (f32[64,8,128]{2,1,0:T(8,128)S(1)}, f32[64,8,128]{2,1,0:T(8,128)S(1)}, u32[]{:S(2)}, u32[]{:S(2)}) collective-permute-start(f32[64,8,128]{2,1,0:T(8,128)S(1)} %get-tuple-element.26), channel_id=1, source_target_pairs={{0,8},{8,0},{16,24},{24,16},{32,40},{40,32},{48,56},{56,48},{64,72... | collective-permute-start | bytes 786440 | tf_op jit(solution)/shard_map/ppermute | solution.py:228
  33.3 0.0 copy-start.2
  33.3 0.0 copy-start.3
  33.3 2.1 %collective-permute-start = (f32[7,16,128]{2,1,0:T(8,128)S(1)}, f32[7,16,128]{2,1,0:T(8,128)S(1)}, u32[]{:S(2)}, u32[]{:S(2)}) collective-permute-start(f32[7,16,128]{2,1,0:T(8,128)S(1)} %slice.15), channel_id=1, source_target_pairs={{1,0},{2,1},{3,2},{4,3},{5,4},{6,5},{7,6},{9,8},{10,9},{11,10},{12... | collective-permute-start | bytes 172040 | tf_op jit(solution)/shard_map/ppermute | solution.py:231
  35.3 1.0 %shard_map.65.partial = f32[4,512,256]{2,1,0:T(8,128)S(1)} custom-call(f32[64,16,128]{2,1,0:T(8,128)S(1)} %bitcast.7, bf16[512,512]{1,0:T(8,128)(2,1)S(1)} %get-tuple-element.18.a_high, bf16[512,512]{1,0:T(8,128)(2,1)S(1)} %get-tuple-element.19.a_low), custom_call_target="tpu_custom_call" | custom-call | flops 1073741824 | bytes 4194304 | tf_op jit(solution)/shard_map/pallas_call | solution.py:237
  36.4 0.0 collective-permute-done.1.off
  36.4 0.0 collective-permute-done.2.flip
  36.4 1.9 %collective-permute-start.3 = (f32[7,16,128]{2,1,0:T(8,128)S(1)}, f32[7,16,128]{2,1,0:T(8,128)S(1)}, u32[]{:S(2)}, u32[]{:S(2)}) collective-permute-start(f32[7,16,128]{2,1,0:T(8,128)S(1)} %pad_maximum_fusion), channel_id=1, source_target_pairs={{1,0},{2,1},{3,2},{4,3},{5,4},{6,5},{7,6},{9,8},{10,9},{11,10},{12... | collective-permute-start | bytes 172040 | tf_op jit(solution)/shard_map/ppermute | solution.py:233
  38.4 0.0 copy-done.2
  38.4 0.0 copy-done.3
  38.4 2.0 %shard_map.66 = (f32[4,4,128,256]{3,2,1,0:T(8,128)S(1)}, f32[512,128]{1,0:T(8,128)S(1)}, f32[8,256]{1,0:T(8,128)S(1)}) custom-call(s32[1]{0:T(128)} %bitcast.parity, f32[64,8,128]{2,1,0:T(8,128)S(1)} %collective-permute-done.1.off, f32[64,8,128]{2,1,0:T(8,128)S(1)} %collective-permute-done.2.flip, f32[4,512,256]{2,1,0:T(8,128)S(1)} %shard_map.65.partial, ...), custom_call_target="tpu_custom_call" | custom-call | flops 2147483648 | bytes 8388608 | tf_op jit(solution)/shard_map/pallas_call | solution.py:245
  40.4 0.0 copy-start.5
  40.4 0.0 collective-permute-done.edge_own
  40.4 2.4 %collective-permute-done.3.edge = f32[7,16,128]{2,1,0:T(8,128)S(1)} collective-permute-done((f32[7,16,128]{2,1,0:T(8,128)S(1)}, f32[7,16,128]{2,1,0:T(8,128)S(1)}, u32[]{:S(2)}, u32[]{:S(2)}) %collective-permute-start.3) | collective-permute-done | bytes 57376 | tf_op jit(solution)/shard_map/ppermute | solution.py:233
  42.9 0.7 shard_map.67
  43.6 14.4 %all_to_all.28 = f32[64,2,128]{2,1,0:T(2,128)S(1)} all-to-all(f32[64,2,128]{2,1,0:T(2,128)S(1)} %bitcast.9), channel_id=1, replica_groups={{504,496,488,480,472,464,456,448,440,432,424,416,408,400,392,384,376,36..., dimensions={0} | all-to-all | bytes 131072 | tf_op jit(solution)/shard_map/all_to_all | solution.py:264
  58.0 0.0 copy-done.5
  58.0 0.8 %shard_map.68 = f32[8,4,16,128]{3,2,1,0:T(8,128)S(1)} custom-call(s32[4]{0:T(128)S(1)} %copy-done.5, f32[128,128]{1,0:T(8,128)S(1)} %bitcast.8, f32[4,4,128,256]{3,2,1,0:T(8,128)S(1)} %get-tuple-element.23.refs_2_, f32[4,128,128]{2,1,0:T(8,128)S(1)} %get-tuple-element.24.refs_3_), custom_call_target="tpu_custom_call" | custom-call | bytes 4194304 | tf_op jit(solution)/shard_map/pallas_call | solution.py:267
  58.9 18.3 %all_to_all.29 = f32[8,4,16,128]{3,2,1,0:T(8,128)S(1)} all-to-all(f32[8,4,16,128]{3,2,1,0:T(8,128)S(1)} %shard_map.68), channel_id=1, replica_groups={{7,6,5,4,3,2,1,0},{15,14,13,12,11,10,9,8},{23,22,21,20,19,18,17,16},{31..., dimensions={0} | all-to-all | bytes 524288 | tf_op jit(solution)/shard_map/all_to_all | solution.py:274
  77.2 0.6 reduce_max.9
  (5 shorter events, 0.1 us)
Async XLA Ops:
  0.0 27.8 %all-to-all-start = ((f32[1,1024,128]{2,0,1:T(1,128)}), f32[1,1024,128]{2,0,1:T(1,128)S(1)}, u32[]{:S(2)}, u32[]{:S(2)}) async-start(f32[1,1024,128]{2,0,1:T(1,128)} %bitcast.10), calls=%async_computation | async-start | bytes 1048576 | tf_op jit(solution)/shard_map/all_to_all | solution.py:214
  10.6 1.0 %copy-start = (bf16[512,512]{1,0:T(8,128)(2,1)S(1)}, bf16[512,512]{1,0:T(8,128)(2,1)}, u32[]{:S(2)}) copy-start(bf16[512,512]{1,0:T(8,128)(2,1)} %constant.31.clone.low_in) | copy-start | bytes 1572868
  11.6 1.0 %copy-start.1 = (bf16[512,512]{1,0:T(8,128)(2,1)S(1)}, bf16[512,512]{1,0:T(8,128)(2,1)}, u32[]{:S(2)}) copy-start(bf16[512,512]{1,0:T(8,128)(2,1)} %constant.30.clone.high_in) | copy-start | bytes 1572868
  12.7 0.7 copy-start.4
  27.8 8.6 %collective-permute-start.1 = (f32[64,8,128]{2,1,0:T(8,128)S(1)}, f32[64,8,128]{2,1,0:T(8,128)S(1)}, u32[]{:S(2)}, u32[]{:S(2)}) collective-permute-start(f32[64,8,128]{2,1,0:T(8,128)S(1)} %get-tuple-element.25), channel_id=1, source_target_pairs={{8,16},{24,32},{40,48},{56,64},{72,80},{88,96},{104,112},{120,128}... | collective-permute-start | bytes 786440 | tf_op jit(solution)/shard_map/ppermute | solution.py:227
  28.5 7.9 %collective-permute-start.2 = (f32[64,8,128]{2,1,0:T(8,128)S(1)}, f32[64,8,128]{2,1,0:T(8,128)S(1)}, u32[]{:S(2)}, u32[]{:S(2)}) collective-permute-start(f32[64,8,128]{2,1,0:T(8,128)S(1)} %get-tuple-element.26), channel_id=1, source_target_pairs={{0,8},{8,0},{16,24},{24,16},{32,40},{40,32},{48,56},{56,48},{64,72... | collective-permute-start | bytes 786440 | tf_op jit(solution)/shard_map/ppermute | solution.py:228
  33.3 5.1 %copy-start.2 = (bf16[4,256,256]{2,1,0:T(8,128)(2,1)S(1)}, bf16[4,256,256]{2,1,0:T(8,128)(2,1)}, u32[]{:S(2)}) copy-start(bf16[4,256,256]{2,1,0:T(8,128)(2,1)} %constant.33.clone.h_low) | copy-start | bytes 1572868
  33.3 5.1 %copy-start.3 = (bf16[4,256,256]{2,1,0:T(8,128)(2,1)S(1)}, bf16[4,256,256]{2,1,0:T(8,128)(2,1)}, u32[]{:S(2)}) copy-start(bf16[4,256,256]{2,1,0:T(8,128)(2,1)} %constant.32.clone.h_high) | copy-start | bytes 1572868
  33.3 7.2 %collective-permute-start = (f32[7,16,128]{2,1,0:T(8,128)S(1)}, f32[7,16,128]{2,1,0:T(8,128)S(1)}, u32[]{:S(2)}, u32[]{:S(2)}) collective-permute-start(f32[7,16,128]{2,1,0:T(8,128)S(1)} %slice.15), channel_id=1, source_target_pairs={{1,0},{2,1},{3,2},{4,3},{5,4},{6,5},{7,6},{9,8},{10,9},{11,10},{12... | collective-permute-start | bytes 172040 | tf_op jit(solution)/shard_map/ppermute | solution.py:231
  36.4 6.4 %collective-permute-start.3 = (f32[7,16,128]{2,1,0:T(8,128)S(1)}, f32[7,16,128]{2,1,0:T(8,128)S(1)}, u32[]{:S(2)}, u32[]{:S(2)}) collective-permute-start(f32[7,16,128]{2,1,0:T(8,128)S(1)} %pad_maximum_fusion), channel_id=1, source_target_pairs={{1,0},{2,1},{3,2},{4,3},{5,4},{6,5},{7,6},{9,8},{10,9},{11,10},{12... | collective-permute-start | bytes 172040 | tf_op jit(solution)/shard_map/ppermute | solution.py:233
  40.4 17.6 %copy-start.5 = (s32[4]{0:T(128)S(1)}, s32[4]{0:T(128)}, u32[]{:S(2)}) copy-start(s32[4]{0:T(128)} %refs_0_.1) | copy-start | bytes 52

commit v7 on v6

--- a/solution.py
+++ b/solution.py
@@ -84,7 +84,13 @@
     return jnp.sum((values * values).reshape(GROUP, ROWS, values.shape[1]), axis=1)
 
 
-def mask_kernel(widths, high_in, low_in, high, low):
+def mask_kernel(per_kernel, widths, high_in, low_in, high, low, floor):
+    index = lax.broadcasted_iota(jnp.int32, (2, NX), 0) * NX + lax.broadcasted_iota(jnp.int32, (2, NX), 1)
+    kernel = jnp.where(index < KERNELS * per_kernel, index // per_kernel, (index - KERNELS * per_kernel) // GROUP)
+    width = jnp.full((2, NX), widths[0], jnp.int32)
+    for k in range(1, KERNELS):
+        width = jnp.where(kernel == k, widths[k], width)
+    floor[...] = width.astype(F32) * EPSILON
     shape = (BLOCK, 2 * DEPTH)
     column = lax.broadcasted_iota(jnp.int32, shape, 1) % DEPTH
     offset = column // ROWS - lax.broadcasted_iota(jnp.int32, shape, 0) // ROWS
@@ -164,19 +170,14 @@
     sums[...] = jnp.where(lax.broadcasted_iota(jnp.int32, sums.shape, 0) % 2 == 0, low, high)
 
 
-def peak_kernel(cells, copies, widths, received, smoothed, last, peaks, scale):
+def peak_kernel(cells, copies, floor, received, smoothed, last, peaks, scale):
     groups = 2 * smoothed.shape[1]
     per_kernel = (groups - 1) * GROUP
     total = jnp.sum(received[...].reshape(-1, 8, NX), axis=0)
     total = total[0:2] + total[2:4] + (total[4:6] + total[6:8])
+    inverse = 1.0 / jnp.sqrt(total * (1.0 / cells) + floor[...])
     for h in (0, 1):
-        index = h * NX + lax.broadcasted_iota(jnp.int32, (1, NX), 1)
-        kernel = jnp.where(index < KERNELS * per_kernel, index // per_kernel, (index - KERNELS * per_kernel) // GROUP)
-        width = jnp.full((1, NX), widths[0], jnp.int32)
-        for k in range(1, KERNELS):
-            width = jnp.where(kernel == k, widths[k], width)
-        inverse = 1.0 / jnp.sqrt(total[h : h + 1] * (1.0 / cells) + width.astype(F32) * EPSILON)
-        scale[h * NX : (h + 1) * NX, :] = jnp.broadcast_to(inverse, (NX, NX)).T
+        scale[h * NX : (h + 1) * NX, :] = jnp.broadcast_to(inverse[h : h + 1], (NX, NX)).T
     for k in range(KERNELS):
         best = None
         for group in range(groups):
@@ -218,7 +219,12 @@
     a_high, a_low = map(jnp.asarray, split(vertical_matrix()))
     h_high, h_low = map(jnp.asarray, split(horizontal_matrices()))
     a_shape = shape(a_high.shape, BF)
-    a_high, a_low = call(mask_kernel, [a_shape, a_shape], [SMEM, VMEM, VMEM], moved=2**21)(widths, a_high, a_low)
+    a_high, a_low, floor = call(
+        lambda *refs: mask_kernel(channels - GROUP, *refs),
+        [a_shape, a_shape, shape((2, NX), F32)],
+        [SMEM, VMEM, VMEM],
+        moved=2**21,
+    )(widths, a_high, a_low)
     own, a_high, a_low = lax.optimization_barrier((own, a_high, a_low))
 
     odd = parity[0] == 1
@@ -262,15 +268,15 @@
         moved=2**20,
     )(parity, edge_own, edge, *matrices, rest, sums)
     received = lax.all_to_all(
-        sums, "tile", split_axis=0, concat_axis=0, tiled=True, axis_index_groups=[list(range(tiles))[::-1]]
+        sums, "tile", split_axis=0, concat_axis=0, tiled=True, axis_index_groups=[[(3 * tiles // 4 - 1 - i) % tiles for i in range(tiles)]]
     )
     peaks = call(
         lambda *refs: peak_kernel(cells, blocks, *refs),
         shape((blocks, KERNELS, ROWS, NX), F32),
-        [SMEM] + [VMEM] * 3,
+        [VMEM] * 4,
         [pltpu.VMEM((KERNELS * channels, NX), F32)],
         moved=2**22,
-    )(widths, received, smoothed, last)
+    )(floor, received, smoothed, last)
     peaks = lax.all_to_all(
         peaks, "fblk", split_axis=0, concat_axis=0, tiled=True, axis_index_groups=[list(range(blocks))[::-1]]
     )

time: 78.3 us -> 77.7 us (level)
    unnamed x12 -> x10, local copies, waits for them, and re-layouts: 2.75 us -> 2.75 us
where the time goes in v7:
time: 77.7 us; the launch traced here: 77.2 us
  blocking collectives  32.6 us (42%)
  starting transfers between devices  20 us (26%)
  waiting for transfers between devices  16.1 us (21%)
  Pallas kernels  4.94 us (6%)
  local copies, waits for them, and re-layouts  2.76 us (4%)
    all_to_all x1, blocking collectives, body(): lax.all_to_all(peaks, 'fblk', split_axis=0, concat_axis=0, tiled=True, ax...  18.3 us
    all_to_all x1, blocking collectives, body(): lax.all_to_all(sums, 'tile', split_axis=0, concat_axis=0, tiled=True, axi...  14.4 us
    all_to_all x1, waiting for transfers between devices, body(): lax.all_to_all(planes, 'tile', split_axis=1, concat_axis=0, tiled=True)  13.6 us
    all_to_all x1, starting transfers between devices, body(): lax.all_to_all(planes, 'tile', split_axis=1, concat_axis=0, tiled=True)  10.6 us
    ppermute x1, starting transfers between devices, body(): lax.ppermute(jnp.where(odd, top, bottom), 'tile', [(i, i ^ 1) for i in ra...  4.74 us
    unnamed x10, local copies, waits for them, and re-layouts  2.75 us
    ppermute x1, waiting for transfers between devices, body(): edge = lax.ppermute(edge, 'fblk', previous)  2.42 us
    pallas_call x1, Pallas kernels, body(): call(main_kernel, [shape((KERNELS, pairs, BLOCK, 2 * NX), F32), shape((KE...  2.06 us
  transfers between devices with their start and end apart: 5, of which 2 were waited for; matrix products, arithmetic and copies ran while one was open for 0% of the time, Pallas kernels for 5%

profile of v7, /device:TPU:64, one launch (start us, length us, event | category | flops | bytes accessed | tf_op | source)
XLA Modules:
  0.0 77.2 jit_solution(4437455558122323246)
XLA Ops:
  0.0 10.6 %all-to-all-start = ((f32[1,1024,128]{2,0,1:T(1,128)}), f32[1,1024,128]{2,0,1:T(1,128)S(1)}, u32[]{:S(2)}, u32[]{:S(2)}) async-start(f32[1,1024,128]{2,0,1:T(1,128)} %bitcast.10), calls=%async_computation | async-start | bytes 1048576 | tf_op jit(solution)/shard_map/all_to_all | solution.py:215
  10.6 0.0 copy-start
  10.6 1.0 %copy-done = bf16[512,512]{1,0:T(8,128)(2,1)S(1)} copy-done((bf16[512,512]{1,0:T(8,128)(2,1)S(1)}, bf16[512,512]{1,0:T(8,128)(2,1)}, u32[]{:S(2)}) %copy-start) | copy-done | bytes 524312
  11.6 0.0 copy-start.1
  11.6 1.0 %copy-done.1 = bf16[512,512]{1,0:T(8,128)(2,1)S(1)} copy-done((bf16[512,512]{1,0:T(8,128)(2,1)S(1)}, bf16[512,512]{1,0:T(8,128)(2,1)}, u32[]{:S(2)}) %copy-start.1) | copy-done | bytes 524312
  12.7 0.0 copy-start.4
  12.7 0.7 copy-done.4
  13.3 0.8 %shard_map.64 = (bf16[512,512]{1,0:T(8,128)(2,1)S(1)}, bf16[512,512]{1,0:T(8,128)(2,1)S(1)}, f32[2,128]{1,0:T(2,128)S(1)}) custom-call(s32[4]{0:T(128)S(1)} %copy-done.4, bf16[512,512]{1,0:T(8,128)(2,1)S(1)} %copy-done.1, bf16[512,512]{1,0:T(8,128)(2,1)S(1)} %copy-done), custom_call_target="tpu_custom_call" | custom-call | bytes 2097152 | tf_op jit(solution)/shard_map/pallas_call | solution.py:222
  14.1 13.6 %all-to-all-done = f32[1,1024,128]{2,0,1:T(1,128)S(1)} async-done(((f32[1,1024,128]{2,0,1:T(1,128)}), f32[1,1024,128]{2,0,1:T(1,128)S(1)}, u32[]{:S(2)}, u32[]{:S(2)}) %all-to-all-start) | async-done | bytes 524320 | tf_op jit(solution)/shard_map/all_to_all | solution.py:215
  27.8 0.7 collective-permute-start.1
  28.5 4.7 %collective-permute-start.2 = (f32[64,8,128]{2,1,0:T(8,128)S(1)}, f32[64,8,128]{2,1,0:T(8,128)S(1)}, u32[]{:S(2)}, u32[]{:S(2)}) collective-permute-start(f32[64,8,128]{2,1,0:T(8,128)S(1)} %get-tuple-element.28), channel_id=1, source_target_pairs={{0,8},{8,0},{16,24},{24,16},{32,40},{40,32},{48,56},{56,48},{64,72... | collective-permute-start | bytes 786440 | tf_op jit(solution)/shard_map/ppermute | solution.py:234
  33.3 0.0 copy-start.2
  33.3 0.0 copy-start.3
  33.3 2.1 %collective-permute-start = (f32[7,16,128]{2,1,0:T(8,128)S(1)}, f32[7,16,128]{2,1,0:T(8,128)S(1)}, u32[]{:S(2)}, u32[]{:S(2)}) collective-permute-start(f32[7,16,128]{2,1,0:T(8,128)S(1)} %slice.15), channel_id=1, source_target_pairs={{1,0},{2,1},{3,2},{4,3},{5,4},{6,5},{7,6},{9,8},{10,9},{11,10},{12... | collective-permute-start | bytes 172040 | tf_op jit(solution)/shard_map/ppermute | solution.py:237
  35.3 1.0 %shard_map.65.partial = f32[4,512,256]{2,1,0:T(8,128)S(1)} custom-call(f32[64,16,128]{2,1,0:T(8,128)S(1)} %bitcast.7, bf16[512,512]{1,0:T(8,128)(2,1)S(1)} %get-tuple-element.20.a_high, bf16[512,512]{1,0:T(8,128)(2,1)S(1)} %get-tuple-element.21.a_low), custom_call_target="tpu_custom_call" | custom-call | flops 1073741824 | bytes 4194304 | tf_op jit(solution)/shard_map/pallas_call | solution.py:243
  36.4 0.0 collective-permute-done.1.off
  36.4 0.0 collective-permute-done.2.flip
  36.4 1.9 %collective-permute-start.3 = (f32[7,16,128]{2,1,0:T(8,128)S(1)}, f32[7,16,128]{2,1,0:T(8,128)S(1)}, u32[]{:S(2)}, u32[]{:S(2)}) collective-permute-start(f32[7,16,128]{2,1,0:T(8,128)S(1)} %pad_maximum_fusion), channel_id=1, source_target_pairs={{1,0},{2,1},{3,2},{4,3},{5,4},{6,5},{7,6},{9,8},{10,9},{11,10},{12... | collective-permute-start | bytes 172040 | tf_op jit(solution)/shard_map/ppermute | solution.py:239
  38.4 0.0 copy-done.2
  38.4 0.0 copy-done.3
  38.4 2.1 %shard_map.66 = (f32[4,4,128,256]{3,2,1,0:T(8,128)S(1)}, f32[512,128]{1,0:T(8,128)S(1)}, f32[8,256]{1,0:T(8,128)S(1)}) custom-call(s32[1]{0:T(128)} %bitcast.parity, f32[64,8,128]{2,1,0:T(8,128)S(1)} %collective-permute-done.1.off, f32[64,8,128]{2,1,0:T(8,128)S(1)} %collective-permute-done.2.flip, f32[4,512,256]{2,1,0:T(8,128)S(1)} %shard_map.65.partial, ...), custom_call_target="tpu_custom_call" | custom-call | flops 2147483648 | bytes 8388608 | tf_op jit(solution)/shard_map/pallas_call | solution.py:251
  40.5 0.0 collective-permute-done.edge_own
  40.5 2.4 %collective-permute-done.3.edge = f32[7,16,128]{2,1,0:T(8,128)S(1)} collective-permute-done((f32[7,16,128]{2,1,0:T(8,128)S(1)}, f32[7,16,128]{2,1,0:T(8,128)S(1)}, u32[]{:S(2)}, u32[]{:S(2)}) %collective-permute-start.3) | collective-permute-done | bytes 57376 | tf_op jit(solution)/shard_map/ppermute | solution.py:239
  42.9 0.7 shard_map.67
  43.6 14.4 %all_to_all.28 = f32[64,2,128]{2,1,0:T(2,128)S(1)} all-to-all(f32[64,2,128]{2,1,0:T(2,128)S(1)} %bitcast.9), channel_id=1, replica_groups={{376,368,360,352,344,336,328,320,312,304,296,288,280,272,264,256,248,24..., dimensions={0} | all-to-all | bytes 131072 | tf_op jit(solution)/shard_map/all_to_all | solution.py:270
  58.0 0.3 shard_map.68
  58.3 18.3 %all_to_all.29 = f32[8,4,16,128]{3,2,1,0:T(8,128)S(1)} all-to-all(f32[8,4,16,128]{3,2,1,0:T(8,128)S(1)} %shard_map.68), channel_id=1, replica_groups={{7,6,5,4,3,2,1,0},{15,14,13,12,11,10,9,8},{23,22,21,20,19,18,17,16},{31..., dimensions={0} | all-to-all | bytes 524288 | tf_op jit(solution)/shard_map/all_to_all | solution.py:280
  76.6 0.6 reduce_max.9
  (5 shorter events, 0.1 us)
Async XLA Ops:
  0.0 27.8 %all-to-all-start = ((f32[1,1024,128]{2,0,1:T(1,128)}), f32[1,1024,128]{2,0,1:T(1,128)S(1)}, u32[]{:S(2)}, u32[]{:S(2)}) async-start(f32[1,1024,128]{2,0,1:T(1,128)} %bitcast.10), calls=%async_computation | async-start | bytes 1048576 | tf_op jit(solution)/shard_map/all_to_all | solution.py:215
  10.6 1.0 %copy-start = (bf16[512,512]{1,0:T(8,128)(2,1)S(1)}, bf16[512,512]{1,0:T(8,128)(2,1)}, u32[]{:S(2)}) copy-start(bf16[512,512]{1,0:T(8,128)(2,1)} %constant.31.clone.refs_2_) | copy-start | bytes 1572868
  11.6 1.0 %copy-start.1 = (bf16[512,512]{1,0:T(8,128)(2,1)S(1)}, bf16[512,512]{1,0:T(8,128)(2,1)}, u32[]{:S(2)}) copy-start(bf16[512,512]{1,0:T(8,128)(2,1)} %constant.30.clone.refs_1_) | copy-start | bytes 1572868
  12.7 0.7 copy-start.4
  27.8 8.6 %collective-permute-start.1 = (f32[64,8,128]{2,1,0:T(8,128)S(1)}, f32[64,8,128]{2,1,0:T(8,128)S(1)}, u32[]{:S(2)}, u32[]{:S(2)}) collective-permute-start(f32[64,8,128]{2,1,0:T(8,128)S(1)} %get-tuple-element.27), channel_id=1, source_target_pairs={{8,16},{24,32},{40,48},{56,64},{72,80},{88,96},{104,112},{120,128}... | collective-permute-start | bytes 786440 | tf_op jit(solution)/shard_map/ppermute | solution.py:233
  28.5 7.9 %collective-permute-start.2 = (f32[64,8,128]{2,1,0:T(8,128)S(1)}, f32[64,8,128]{2,1,0:T(8,128)S(1)}, u32[]{:S(2)}, u32[]{:S(2)}) collective-permute-start(f32[64,8,128]{2,1,0:T(8,128)S(1)} %get-tuple-element.28), channel_id=1, source_target_pairs={{0,8},{8,0},{16,24},{24,16},{32,40},{40,32},{48,56},{56,48},{64,72... | collective-permute-start | bytes 786440 | tf_op jit(solution)/shard_map/ppermute | solution.py:234
  33.3 5.1 %copy-start.2 = (bf16[4,256,256]{2,1,0:T(8,128)(2,1)S(1)}, bf16[4,256,256]{2,1,0:T(8,128)(2,1)}, u32[]{:S(2)}) copy-start(bf16[4,256,256]{2,1,0:T(8,128)(2,1)} %constant.33.clone.h_low) | copy-start | bytes 1572868
  33.3 5.1 %copy-start.3 = (bf16[4,256,256]{2,1,0:T(8,128)(2,1)S(1)}, bf16[4,256,256]{2,1,0:T(8,128)(2,1)}, u32[]{:S(2)}) copy-start(bf16[4,256,256]{2,1,0:T(8,128)(2,1)} %constant.32.clone.h_high) | copy-start | bytes 1572868
  33.3 7.2 %collective-permute-start = (f32[7,16,128]{2,1,0:T(8,128)S(1)}, f32[7,16,128]{2,1,0:T(8,128)S(1)}, u32[]{:S(2)}, u32[]{:S(2)}) collective-permute-start(f32[7,16,128]{2,1,0:T(8,128)S(1)} %slice.15), channel_id=1, source_target_pairs={{1,0},{2,1},{3,2},{4,3},{5,4},{6,5},{7,6},{9,8},{10,9},{11,10},{12... | collective-permute-start | bytes 172040 | tf_op jit(solution)/shard_map/ppermute | solution.py:237
  36.4 6.4 %collective-permute-start.3 = (f32[7,16,128]{2,1,0:T(8,128)S(1)}, f32[7,16,128]{2,1,0:T(8,128)S(1)}, u32[]{:S(2)}, u32[]{:S(2)}) collective-permute-start(f32[7,16,128]{2,1,0:T(8,128)S(1)} %pad_maximum_fusion), channel_id=1, source_target_pairs={{1,0},{2,1},{3,2},{4,3},{5,4},{6,5},{7,6},{9,8},{10,9},{11,10},{12... | collective-permute-start | bytes 172040 | tf_op jit(solution)/shard_map/ppermute | solution.py:239

commit v8 on v7

--- a/solution.py
+++ b/solution.py
@@ -165,9 +165,9 @@
         smoothed[k] = z
         squares.append(row_squares(z))
     total = lane_sums(jnp.concatenate(squares, axis=0))
-    low = jnp.broadcast_to(main_sums[0:1, :NX], sums.shape)
-    high = jnp.broadcast_to(main_sums[0:1, NX:] + total[0:1], sums.shape)
-    sums[...] = jnp.where(lax.broadcasted_iota(jnp.int32, sums.shape, 0) % 2 == 0, low, high)
+    odd = lax.broadcasted_iota(jnp.int32, (8, NX), 0) & 1
+    both = jnp.where(odd == 0, main_sums[:, :NX], main_sums[:, NX:] + total)
+    sums[...] = jnp.concatenate([both] * (sums.shape[0] // 8), axis=0)
 
 
 def peak_kernel(cells, copies, floor, received, smoothed, last, peaks, scale):

time: 77.7 us -> 77.6 us (level)
  no operation moved by 1% of the time
where the time goes in v8:
time: 77.6 us; the launch traced here: 77.2 us
  blocking collectives  32.6 us (42%)
  starting transfers between devices  20 us (26%)
  waiting for transfers between devices  16.1 us (21%)
  Pallas kernels  4.93 us (6%)
  local copies, waits for them, and re-layouts  2.76 us (4%)
    all_to_all x1, blocking collectives, body(): lax.all_to_all(peaks, 'fblk', split_axis=0, concat_axis=0, tiled=True, ax...  18.3 us
    all_to_all x1, blocking collectives, body(): lax.all_to_all(sums, 'tile', split_axis=0, concat_axis=0, tiled=True, axi...  14.4 us
    all_to_all x1, waiting for transfers between devices, body(): lax.all_to_all(planes, 'tile', split_axis=1, concat_axis=0, tiled=True)  13.6 us
    all_to_all x1, starting transfers between devices, body(): lax.all_to_all(planes, 'tile', split_axis=1, concat_axis=0, tiled=True)  10.6 us
    ppermute x1, starting transfers between devices, body(): lax.ppermute(jnp.where(odd, top, bottom), 'tile', [(i, i ^ 1) for i in ra...  4.74 us
    unnamed x10, local copies, waits for them, and re-layouts  2.75 us
    ppermute x1, waiting for transfers between devices, body(): edge = lax.ppermute(edge, 'fblk', previous)  2.42 us
    pallas_call x1, Pallas kernels, body(): call(main_kernel, [shape((KERNELS, pairs, BLOCK, 2 * NX), F32), shape((KE...  2.06 us
  transfers between devices with their start and end apart: 5, of which 2 were waited for; matrix products, arithmetic and copies ran while one was open for 0% of the time, Pallas kernels for 5%

profile of v8, /device:TPU:64, one launch (start us, length us, event | category | flops | bytes accessed | tf_op | source)
XLA Modules:
  0.0 77.2 jit_solution(152320152985871283)
XLA Ops:
  0.0 10.6 %all-to-all-start = ((f32[1,1024,128]{2,0,1:T(1,128)}), f32[1,1024,128]{2,0,1:T(1,128)S(1)}, u32[]{:S(2)}, u32[]{:S(2)}) async-start(f32[1,1024,128]{2,0,1:T(1,128)} %bitcast.10), calls=%async_computation | async-start | bytes 1048576 | tf_op jit(solution)/shard_map/all_to_all | solution.py:215
  10.6 0.0 copy-start
  10.6 1.0 %copy-done = bf16[512,512]{1,0:T(8,128)(2,1)S(1)} copy-done((bf16[512,512]{1,0:T(8,128)(2,1)S(1)}, bf16[512,512]{1,0:T(8,128)(2,1)}, u32[]{:S(2)}) %copy-start) | copy-done | bytes 524312
  11.6 0.0 copy-start.1
  11.6 1.0 %copy-done.1 = bf16[512,512]{1,0:T(8,128)(2,1)S(1)} copy-done((bf16[512,512]{1,0:T(8,128)(2,1)S(1)}, bf16[512,512]{1,0:T(8,128)(2,1)}, u32[]{:S(2)}) %copy-start.1) | copy-done | bytes 524312
  12.7 0.0 copy-start.4
  12.7 0.7 copy-done.4
  13.3 0.8 %shard_map.64 = (bf16[512,512]{1,0:T(8,128)(2,1)S(1)}, bf16[512,512]{1,0:T(8,128)(2,1)S(1)}, f32[2,128]{1,0:T(2,128)S(1)}) custom-call(s32[4]{0:T(128)S(1)} %copy-done.4, bf16[512,512]{1,0:T(8,128)(2,1)S(1)} %copy-done.1, bf16[512,512]{1,0:T(8,128)(2,1)S(1)} %copy-done), custom_call_target="tpu_custom_call" | custom-call | bytes 2097152 | tf_op jit(solution)/shard_map/pallas_call | solution.py:222
  14.1 13.6 %all-to-all-done = f32[1,1024,128]{2,0,1:T(1,128)S(1)} async-done(((f32[1,1024,128]{2,0,1:T(1,128)}), f32[1,1024,128]{2,0,1:T(1,128)S(1)}, u32[]{:S(2)}, u32[]{:S(2)}) %all-to-all-start) | async-done | bytes 524320 | tf_op jit(solution)/shard_map/all_to_all | solution.py:215
  27.8 0.7 collective-permute-start.1
  28.5 4.7 %collective-permute-start.2 = (f32[64,8,128]{2,1,0:T(8,128)S(1)}, f32[64,8,128]{2,1,0:T(8,128)S(1)}, u32[]{:S(2)}, u32[]{:S(2)}) collective-permute-start(f32[64,8,128]{2,1,0:T(8,128)S(1)} %get-tuple-element.28), channel_id=1, source_target_pairs={{0,8},{8,0},{16,24},{24,16},{32,40},{40,32},{48,56},{56,48},{64,72... | collective-permute-start | bytes 786440 | tf_op jit(solution)/shard_map/ppermute | solution.py:234
  33.3 0.0 copy-start.2
  33.3 0.0 copy-start.3
  33.3 2.1 %collective-permute-start = (f32[7,16,128]{2,1,0:T(8,128)S(1)}, f32[7,16,128]{2,1,0:T(8,128)S(1)}, u32[]{:S(2)}, u32[]{:S(2)}) collective-permute-start(f32[7,16,128]{2,1,0:T(8,128)S(1)} %slice.15), channel_id=1, source_target_pairs={{1,0},{2,1},{3,2},{4,3},{5,4},{6,5},{7,6},{9,8},{10,9},{11,10},{12... | collective-permute-start | bytes 172040 | tf_op jit(solution)/shard_map/ppermute | solution.py:237
  35.3 1.0 %shard_map.65.partial = f32[4,512,256]{2,1,0:T(8,128)S(1)} custom-call(f32[64,16,128]{2,1,0:T(8,128)S(1)} %bitcast.7, bf16[512,512]{1,0:T(8,128)(2,1)S(1)} %get-tuple-element.20.a_high, bf16[512,512]{1,0:T(8,128)(2,1)S(1)} %get-tuple-element.21.a_low), custom_call_target="tpu_custom_call" | custom-call | flops 1073741824 | bytes 4194304 | tf_op jit(solution)/shard_map/pallas_call | solution.py:243
  36.4 0.0 collective-permute-done.1.off
  36.4 0.0 collective-permute-done.2.flip
  36.4 1.9 %collective-permute-start.3 = (f32[7,16,128]{2,1,0:T(8,128)S(1)}, f32[7,16,128]{2,1,0:T(8,128)S(1)}, u32[]{:S(2)}, u32[]{:S(2)}) collective-permute-start(f32[7,16,128]{2,1,0:T(8,128)S(1)} %pad_maximum_fusion), channel_id=1, source_target_pairs={{1,0},{2,1},{3,2},{4,3},{5,4},{6,5},{7,6},{9,8},{10,9},{11,10},{12... | collective-permute-start | bytes 172040 | tf_op jit(solution)/shard_map/ppermute | solution.py:239
  38.4 0.0 copy-done.2
  38.4 0.0 copy-done.3
  38.4 2.1 %shard_map.66 = (f32[4,4,128,256]{3,2,1,0:T(8,128)S(1)}, f32[512,128]{1,0:T(8,128)S(1)}, f32[8,256]{1,0:T(8,128)S(1)}) custom-call(s32[1]{0:T(128)} %bitcast.parity, f32[64,8,128]{2,1,0:T(8,128)S(1)} %collective-permute-done.1.off, f32[64,8,128]{2,1,0:T(8,128)S(1)} %collective-permute-done.2.flip, f32[4,512,256]{2,1,0:T(8,128)S(1)} %shard_map.65.partial, ...), custom_call_target="tpu_custom_call" | custom-call | flops 2147483648 | bytes 8388608 | tf_op jit(solution)/shard_map/pallas_call | solution.py:251
  40.5 0.0 collective-permute-done.edge_own
  40.5 2.4 %collective-permute-done.3.edge = f32[7,16,128]{2,1,0:T(8,128)S(1)} collective-permute-done((f32[7,16,128]{2,1,0:T(8,128)S(1)}, f32[7,16,128]{2,1,0:T(8,128)S(1)}, u32[]{:S(2)}, u32[]{:S(2)}) %collective-permute-start.3) | collective-permute-done | bytes 57376 | tf_op jit(solution)/shard_map/ppermute | solution.py:239
  42.9 0.7 shard_map.67
  43.6 14.4 %all_to_all.28 = f32[64,2,128]{2,1,0:T(2,128)S(1)} all-to-all(f32[64,2,128]{2,1,0:T(2,128)S(1)} %bitcast.9), channel_id=1, replica_groups={{376,368,360,352,344,336,328,320,312,304,296,288,280,272,264,256,248,24..., dimensions={0} | all-to-all | bytes 131072 | tf_op jit(solution)/shard_map/all_to_all | solution.py:270
  58.0 0.3 shard_map.68
  58.3 18.3 %all_to_all.29 = f32[8,4,16,128]{3,2,1,0:T(8,128)S(1)} all-to-all(f32[8,4,16,128]{3,2,1,0:T(8,128)S(1)} %shard_map.68), channel_id=1, replica_groups={{7,6,5,4,3,2,1,0},{15,14,13,12,11,10,9,8},{23,22,21,20,19,18,17,16},{31..., dimensions={0} | all-to-all | bytes 524288 | tf_op jit(solution)/shard_map/all_to_all | solution.py:280
  76.6 0.6 reduce_max.9
  (5 shorter events, 0.1 us)
Async XLA Ops:
  0.0 27.8 %all-to-all-start = ((f32[1,1024,128]{2,0,1:T(1,128)}), f32[1,1024,128]{2,0,1:T(1,128)S(1)}, u32[]{:S(2)}, u32[]{:S(2)}) async-start(f32[1,1024,128]{2,0,1:T(1,128)} %bitcast.10), calls=%async_computation | async-start | bytes 1048576 | tf_op jit(solution)/shard_map/all_to_all | solution.py:215
  10.6 1.0 %copy-start = (bf16[512,512]{1,0:T(8,128)(2,1)S(1)}, bf16[512,512]{1,0:T(8,128)(2,1)}, u32[]{:S(2)}) copy-start(bf16[512,512]{1,0:T(8,128)(2,1)} %constant.31.clone.refs_2_) | copy-start | bytes 1572868
  11.6 1.0 %copy-start.1 = (bf16[512,512]{1,0:T(8,128)(2,1)S(1)}, bf16[512,512]{1,0:T(8,128)(2,1)}, u32[]{:S(2)}) copy-start(bf16[512,512]{1,0:T(8,128)(2,1)} %constant.30.clone.refs_1_) | copy-start | bytes 1572868
  12.7 0.7 copy-start.4
  27.8 8.6 %collective-permute-start.1 = (f32[64,8,128]{2,1,0:T(8,128)S(1)}, f32[64,8,128]{2,1,0:T(8,128)S(1)}, u32[]{:S(2)}, u32[]{:S(2)}) collective-permute-start(f32[64,8,128]{2,1,0:T(8,128)S(1)} %get-tuple-element.27), channel_id=1, source_target_pairs={{8,16},{24,32},{40,48},{56,64},{72,80},{88,96},{104,112},{120,128}... | collective-permute-start | bytes 786440 | tf_op jit(solution)/shard_map/ppermute | solution.py:233
  28.5 7.9 %collective-permute-start.2 = (f32[64,8,128]{2,1,0:T(8,128)S(1)}, f32[64,8,128]{2,1,0:T(8,128)S(1)}, u32[]{:S(2)}, u32[]{:S(2)}) collective-permute-start(f32[64,8,128]{2,1,0:T(8,128)S(1)} %get-tuple-element.28), channel_id=1, source_target_pairs={{0,8},{8,0},{16,24},{24,16},{32,40},{40,32},{48,56},{56,48},{64,72... | collective-permute-start | bytes 786440 | tf_op jit(solution)/shard_map/ppermute | solution.py:234
  33.3 5.1 %copy-start.2 = (bf16[4,256,256]{2,1,0:T(8,128)(2,1)S(1)}, bf16[4,256,256]{2,1,0:T(8,128)(2,1)}, u32[]{:S(2)}) copy-start(bf16[4,256,256]{2,1,0:T(8,128)(2,1)} %constant.33.clone.h_low) | copy-start | bytes 1572868
  33.3 5.1 %copy-start.3 = (bf16[4,256,256]{2,1,0:T(8,128)(2,1)S(1)}, bf16[4,256,256]{2,1,0:T(8,128)(2,1)}, u32[]{:S(2)}) copy-start(bf16[4,256,256]{2,1,0:T(8,128)(2,1)} %constant.32.clone.h_high) | copy-start | bytes 1572868
  33.3 7.2 %collective-permute-start = (f32[7,16,128]{2,1,0:T(8,128)S(1)}, f32[7,16,128]{2,1,0:T(8,128)S(1)}, u32[]{:S(2)}, u32[]{:S(2)}) collective-permute-start(f32[7,16,128]{2,1,0:T(8,128)S(1)} %slice.15), channel_id=1, source_target_pairs={{1,0},{2,1},{3,2},{4,3},{5,4},{6,5},{7,6},{9,8},{10,9},{11,10},{12... | collective-permute-start | bytes 172040 | tf_op jit(solution)/shard_map/ppermute | solution.py:237
  36.4 6.4 %collective-permute-start.3 = (f32[7,16,128]{2,1,0:T(8,128)S(1)}, f32[7,16,128]{2,1,0:T(8,128)S(1)}, u32[]{:S(2)}, u32[]{:S(2)}) collective-permute-start(f32[7,16,128]{2,1,0:T(8,128)S(1)} %pad_maximum_fusion), channel_id=1, source_target_pairs={{1,0},{2,1},{3,2},{4,3},{5,4},{6,5},{7,6},{9,8},{10,9},{11,10},{12... | collective-permute-start | bytes 172040 | tf_op jit(solution)/shard_map/ppermute | solution.py:239

commit v9 on v8

--- a/solution.py
+++ b/solution.py
@@ -161,7 +161,8 @@
     squares = [jnp.zeros((NX - KERNELS * GROUP, NX), F32)]
     for k in range(KERNELS):
         rows = slice(k * BLOCK, (k + 1) * BLOCK)
-        z = dot3(yh[rows], yl[rows], h_high[k, :NX, :NX], h_low[k, :NX, :NX])
+        both = dot(jnp.concatenate([yh[rows], yl[rows]], axis=1), h_high[k])
+        z = both[:, :NX] + (both[:, NX:] + dot(yh[rows], h_low[k, :NX, :NX]))
         smoothed[k] = z
         squares.append(row_squares(z))
     total = lane_sums(jnp.concatenate(squares, axis=0))

time: 77.6 us -> 77.7 us (level)
  no operation moved by 1% of the time
where the time goes in v9:
time: 77.7 us; the launch traced here: 77.2 us
  blocking collectives  32.6 us (42%)
  starting transfers between devices  20 us (26%)
  waiting for transfers between devices  16.1 us (21%)
  Pallas kernels  4.96 us (6%)
  local copies, waits for them, and re-layouts  2.76 us (4%)
    all_to_all x1, blocking collectives, body(): lax.all_to_all(peaks, 'fblk', split_axis=0, concat_axis=0, tiled=True, ax...  18.3 us
    all_to_all x1, blocking collectives, body(): lax.all_to_all(sums, 'tile', split_axis=0, concat_axis=0, tiled=True, axi...  14.4 us
    all_to_all x1, waiting for transfers between devices, body(): lax.all_to_all(planes, 'tile', split_axis=1, concat_axis=0, tiled=True)  13.6 us
    all_to_all x1, starting transfers between devices, body(): lax.all_to_all(planes, 'tile', split_axis=1, concat_axis=0, tiled=True)  10.6 us
    ppermute x1, starting transfers between devices, body(): lax.ppermute(jnp.where(odd, top, bottom), 'tile', [(i, i ^ 1) for i in ra...  4.74 us
    unnamed x10, local copies, waits for them, and re-layouts  2.75 us
    ppermute x1, waiting for transfers between devices, body(): edge = lax.ppermute(edge, 'fblk', previous)  2.42 us
    pallas_call x1, Pallas kernels, body(): call(main_kernel, [shape((KERNELS, pairs, BLOCK, 2 * NX), F32), shape((KE...  2.06 us
  transfers between devices with their start and end apart: 5, of which 2 were waited for; matrix products, arithmetic and copies ran while one was open for 0% of the time, Pallas kernels for 5%

profile of v9, /device:TPU:64, one launch (start us, length us, event | category | flops | bytes accessed | tf_op | source)
XLA Modules:
  0.0 77.2 jit_solution(5463837179248157921)
XLA Ops:
  0.0 10.6 %all-to-all-start = ((f32[1,1024,128]{2,0,1:T(1,128)}), f32[1,1024,128]{2,0,1:T(1,128)S(1)}, u32[]{:S(2)}, u32[]{:S(2)}) async-start(f32[1,1024,128]{2,0,1:T(1,128)} %bitcast.10), calls=%async_computation | async-start | bytes 1048576 | tf_op jit(solution)/shard_map/all_to_all | solution.py:216
  10.6 0.0 copy-start
  10.6 1.0 %copy-done = bf16[512,512]{1,0:T(8,128)(2,1)S(1)} copy-done((bf16[512,512]{1,0:T(8,128)(2,1)S(1)}, bf16[512,512]{1,0:T(8,128)(2,1)}, u32[]{:S(2)}) %copy-start) | copy-done | bytes 524312
  11.6 0.0 copy-start.1
  11.6 1.0 %copy-done.1 = bf16[512,512]{1,0:T(8,128)(2,1)S(1)} copy-done((bf16[512,512]{1,0:T(8,128)(2,1)S(1)}, bf16[512,512]{1,0:T(8,128)(2,1)}, u32[]{:S(2)}) %copy-start.1) | copy-done | bytes 524312
  12.7 0.0 copy-start.4
  12.7 0.7 copy-done.4
  13.3 0.8 %shard_map.64 = (bf16[512,512]{1,0:T(8,128)(2,1)S(1)}, bf16[512,512]{1,0:T(8,128)(2,1)S(1)}, f32[2,128]{1,0:T(2,128)S(1)}) custom-call(s32[4]{0:T(128)S(1)} %copy-done.4, bf16[512,512]{1,0:T(8,128)(2,1)S(1)} %copy-done.1, bf16[512,512]{1,0:T(8,128)(2,1)S(1)} %copy-done), custom_call_target="tpu_custom_call" | custom-call | bytes 2097152 | tf_op jit(solution)/shard_map/pallas_call | solution.py:223
  14.1 13.6 %all-to-all-done = f32[1,1024,128]{2,0,1:T(1,128)S(1)} async-done(((f32[1,1024,128]{2,0,1:T(1,128)}), f32[1,1024,128]{2,0,1:T(1,128)S(1)}, u32[]{:S(2)}, u32[]{:S(2)}) %all-to-all-start) | async-done | bytes 524320 | tf_op jit(solution)/shard_map/all_to_all | solution.py:216
  27.8 0.7 collective-permute-start.1
  28.5 4.7 %collective-permute-start.2 = (f32[64,8,128]{2,1,0:T(8,128)S(1)}, f32[64,8,128]{2,1,0:T(8,128)S(1)}, u32[]{:S(2)}, u32[]{:S(2)}) collective-permute-start(f32[64,8,128]{2,1,0:T(8,128)S(1)} %get-tuple-element.28), channel_id=1, source_target_pairs={{0,8},{8,0},{16,24},{24,16},{32,40},{40,32},{48,56},{56,48},{64,72... | collective-permute-start | bytes 786440 | tf_op jit(solution)/shard_map/ppermute | solution.py:235
  33.3 0.0 copy-start.2
  33.3 0.0 copy-start.3
  33.3 2.1 %collective-permute-start = (f32[7,16,128]{2,1,0:T(8,128)S(1)}, f32[7,16,128]{2,1,0:T(8,128)S(1)}, u32[]{:S(2)}, u32[]{:S(2)}) collective-permute-start(f32[7,16,128]{2,1,0:T(8,128)S(1)} %slice.15), channel_id=1, source_target_pairs={{1,0},{2,1},{3,2},{4,3},{5,4},{6,5},{7,6},{9,8},{10,9},{11,10},{12... | collective-permute-start | bytes 172040 | tf_op jit(solution)/shard_map/ppermute | solution.py:238
  35.3 1.0 %shard_map.65.partial = f32[4,512,256]{2,1,0:T(8,128)S(1)} custom-call(f32[64,16,128]{2,1,0:T(8,128)S(1)} %bitcast.7, bf16[512,512]{1,0:T(8,128)(2,1)S(1)} %get-tuple-element.20.a_high, bf16[512,512]{1,0:T(8,128)(2,1)S(1)} %get-tuple-element.21.a_low), custom_call_target="tpu_custom_call" | custom-call | flops 1073741824 | bytes 4194304 | tf_op jit(solution)/shard_map/pallas_call | solution.py:244
  36.4 0.0 collective-permute-done.1.off
  36.4 0.0 collective-permute-done.2.flip
  36.4 1.9 %collective-permute-start.3 = (f32[7,16,128]{2,1,0:T(8,128)S(1)}, f32[7,16,128]{2,1,0:T(8,128)S(1)}, u32[]{:S(2)}, u32[]{:S(2)}) collective-permute-start(f32[7,16,128]{2,1,0:T(8,128)S(1)} %pad_maximum_fusion), channel_id=1, source_target_pairs={{1,0},{2,1},{3,2},{4,3},{5,4},{6,5},{7,6},{9,8},{10,9},{11,10},{12... | collective-permute-start | bytes 172040 | tf_op jit(solution)/shard_map/ppermute | solution.py:240
  38.4 0.0 copy-done.2
  38.4 0.0 copy-done.3
  38.4 2.1 %shard_map.66 = (f32[4,4,128,256]{3,2,1,0:T(8,128)S(1)}, f32[512,128]{1,0:T(8,128)S(1)}, f32[8,256]{1,0:T(8,128)S(1)}) custom-call(s32[1]{0:T(128)} %bitcast.parity, f32[64,8,128]{2,1,0:T(8,128)S(1)} %collective-permute-done.1.off, f32[64,8,128]{2,1,0:T(8,128)S(1)} %collective-permute-done.2.flip, f32[4,512,256]{2,1,0:T(8,128)S(1)} %shard_map.65.partial, ...), custom_call_target="tpu_custom_call" | custom-call | flops 2147483648 | bytes 8388608 | tf_op jit(solution)/shard_map/pallas_call | solution.py:252
  40.5 0.0 collective-permute-done.edge_own
  40.5 2.4 %collective-permute-done.3.edge = f32[7,16,128]{2,1,0:T(8,128)S(1)} collective-permute-done((f32[7,16,128]{2,1,0:T(8,128)S(1)}, f32[7,16,128]{2,1,0:T(8,128)S(1)}, u32[]{:S(2)}, u32[]{:S(2)}) %collective-permute-start.3) | collective-permute-done | bytes 57376 | tf_op jit(solution)/shard_map/ppermute | solution.py:240
  42.9 0.8 shard_map.67
  43.6 14.4 %all_to_all.28 = f32[64,2,128]{2,1,0:T(2,128)S(1)} all-to-all(f32[64,2,128]{2,1,0:T(2,128)S(1)} %bitcast.9), channel_id=1, replica_groups={{376,368,360,352,344,336,328,320,312,304,296,288,280,272,264,256,248,24..., dimensions={0} | all-to-all | bytes 131072 | tf_op jit(solution)/shard_map/all_to_all | solution.py:271
  58.0 0.3 shard_map.68
  58.3 18.3 %all_to_all.29 = f32[8,4,16,128]{3,2,1,0:T(8,128)S(1)} all-to-all(f32[8,4,16,128]{3,2,1,0:T(8,128)S(1)} %shard_map.68), channel_id=1, replica_groups={{7,6,5,4,3,2,1,0},{15,14,13,12,11,10,9,8},{23,22,21,20,19,18,17,16},{31..., dimensions={0} | all-to-all | bytes 524288 | tf_op jit(solution)/shard_map/all_to_all | solution.py:281
  76.6 0.6 reduce_max.9
  (5 shorter events, 0.1 us)
Async XLA Ops:
  0.0 27.8 %all-to-all-start = ((f32[1,1024,128]{2,0,1:T(1,128)}), f32[1,1024,128]{2,0,1:T(1,128)S(1)}, u32[]{:S(2)}, u32[]{:S(2)}) async-start(f32[1,1024,128]{2,0,1:T(1,128)} %bitcast.10), calls=%async_computation | async-start | bytes 1048576 | tf_op jit(solution)/shard_map/all_to_all | solution.py:216
  10.6 1.0 %copy-start = (bf16[512,512]{1,0:T(8,128)(2,1)S(1)}, bf16[512,512]{1,0:T(8,128)(2,1)}, u32[]{:S(2)}) copy-start(bf16[512,512]{1,0:T(8,128)(2,1)} %constant.31.clone.refs_2_) | copy-start | bytes 1572868
  11.6 1.0 %copy-start.1 = (bf16[512,512]{1,0:T(8,128)(2,1)S(1)}, bf16[512,512]{1,0:T(8,128)(2,1)}, u32[]{:S(2)}) copy-start(bf16[512,512]{1,0:T(8,128)(2,1)} %constant.30.clone.refs_1_) | copy-start | bytes 1572868
  12.7 0.7 copy-start.4
  27.8 8.6 %collective-permute-start.1 = (f32[64,8,128]{2,1,0:T(8,128)S(1)}, f32[64,8,128]{2,1,0:T(8,128)S(1)}, u32[]{:S(2)}, u32[]{:S(2)}) collective-permute-start(f32[64,8,128]{2,1,0:T(8,128)S(1)} %get-tuple-element.27), channel_id=1, source_target_pairs={{8,16},{24,32},{40,48},{56,64},{72,80},{88,96},{104,112},{120,128}... | collective-permute-start | bytes 786440 | tf_op jit(solution)/shard_map/ppermute | solution.py:234
  28.5 7.9 %collective-permute-start.2 = (f32[64,8,128]{2,1,0:T(8,128)S(1)}, f32[64,8,128]{2,1,0:T(8,128)S(1)}, u32[]{:S(2)}, u32[]{:S(2)}) collective-permute-start(f32[64,8,128]{2,1,0:T(8,128)S(1)} %get-tuple-element.28), channel_id=1, source_target_pairs={{0,8},{8,0},{16,24},{24,16},{32,40},{40,32},{48,56},{56,48},{64,72... | collective-permute-start | bytes 786440 | tf_op jit(solution)/shard_map/ppermute | solution.py:235
  33.3 5.1 %copy-start.2 = (bf16[4,256,256]{2,1,0:T(8,128)(2,1)S(1)}, bf16[4,256,256]{2,1,0:T(8,128)(2,1)}, u32[]{:S(2)}) copy-start(bf16[4,256,256]{2,1,0:T(8,128)(2,1)} %constant.33.clone.h_low) | copy-start | bytes 1572868
  33.3 5.1 %copy-start.3 = (bf16[4,256,256]{2,1,0:T(8,128)(2,1)S(1)}, bf16[4,256,256]{2,1,0:T(8,128)(2,1)}, u32[]{:S(2)}) copy-start(bf16[4,256,256]{2,1,0:T(8,128)(2,1)} %constant.32.clone.h_high) | copy-start | bytes 1572868
  33.3 7.2 %collective-permute-start = (f32[7,16,128]{2,1,0:T(8,128)S(1)}, f32[7,16,128]{2,1,0:T(8,128)S(1)}, u32[]{:S(2)}, u32[]{:S(2)}) collective-permute-start(f32[7,16,128]{2,1,0:T(8,128)S(1)} %slice.15), channel_id=1, source_target_pairs={{1,0},{2,1},{3,2},{4,3},{5,4},{6,5},{7,6},{9,8},{10,9},{11,10},{12... | collective-permute-start | bytes 172040 | tf_op jit(solution)/shard_map/ppermute | solution.py:238
  36.4 6.4 %collective-permute-start.3 = (f32[7,16,128]{2,1,0:T(8,128)S(1)}, f32[7,16,128]{2,1,0:T(8,128)S(1)}, u32[]{:S(2)}, u32[]{:S(2)}) collective-permute-start(f32[7,16,128]{2,1,0:T(8,128)S(1)} %pad_maximum_fusion), channel_id=1, source_target_pairs={{1,0},{2,1},{3,2},{4,3},{5,4},{6,5},{7,6},{9,8},{10,9},{11,10},{12... | collective-permute-start | bytes 172040 | tf_op jit(solution)/shard_map/ppermute | solution.py:240
